TPU v7x, 512 devices: a whole 4x8x8 slice. The times are simulated.
512 devices in a mesh: outer: 32 (over y, z_lo), inner: 16 (over x, z_hi, core).
Axes of the slice: x: 4, y: 8, z: 8 (z_hi: 2, z_lo: 4; z = z_hi * 4 + z_lo), core: 2. Of those that a mesh axis runs over, the one named last changes fastest.
Arguments:
- image_emb: bfloat16 [65536, 1152], P(('outer', 'inner')), may hold values from -0.4375 to 0.4375
- text_emb: bfloat16 [65536, 1152], P(('outer', 'inner')), may hold values from -0.4375 to 0.4375
- log_scale: float32 [1], replicated, may hold values from 1.8 to 2.8
- bias: float32 [1], replicated, may hold values from -5 to -3
Outputs:
- image_loss: float32 [65536], P(('outer', 'inner'))
- grad_image: float32 [65536, 1152], P(('outer', 'inner'))
- grad_text: float32 [65536, 1152], P(('outer', 'inner'))
All inputs are finite; a program needn't handle non-finite values.
Results may differ from a plain program's by a relative error of at most 0.0042.
Values may be sent and summed in bfloat16 or wider, within the bound.
A program may use at most 64 MiB of HBM per device.

v0:
```python
import jax
import jax.numpy as jnp
from jax import lax
from jax.sharding import PartitionSpec as P

REACH = 1


EPS = 1e-06


def passed_along(value, axis, by):
    length = lax.axis_size(axis)
    return lax.ppermute(value, axis, [(i, (i + by) % length) for i in range(length)])


def normalize(raw):
    wide = raw.astype(jnp.float32)
    inverse = lax.rsqrt(jnp.sum(wide * wide, axis=1, keepdims=True) + EPS)
    unit = wide * inverse
    return (unit, inverse, unit.astype(jnp.bfloat16))


def tile_terms(block, partners, positive, scale, offset):
    dots = lax.dot_general(
        block, partners, (((1,), (1,)), ((), ())), preferred_element_type=jnp.float32
    )
    logits = scale * dots + offset
    signed = jnp.where(positive, logits, -logits)
    losses = jnp.sum(jax.nn.softplus(-signed), axis=1)
    weights = (jax.nn.sigmoid(logits) - positive.astype(jnp.float32)).astype(jnp.bfloat16)
    grads = scale * jnp.dot(weights, partners, preferred_element_type=jnp.float32)
    return (losses, grads)


def backprop(unit, inverse, grads):
    return (grads - unit * jnp.sum(unit * grads, axis=1, keepdims=True)) * inverse


def cycle_pass(own, partners, matches, scale, offset):
    local_n = own.shape[0]
    width = own.shape[1]
    steps_n = 2 * REACH + 1
    nothing = jnp.zeros(matches.shape, dtype=bool)
    block = passed_along(own, "outer", -REACH)
    grad_acc = jnp.zeros((local_n, width), jnp.float32)
    loss_acc = jnp.zeros((local_n,), jnp.float32)
    for turn in range(steps_n):
        positive = matches if turn == REACH else nothing
        losses, grads = tile_terms(block, partners, positive, scale, offset)
        grad_acc = grad_acc + grads
        loss_acc = loss_acc + losses
        if turn < steps_n - 1:
            block = passed_along(block, "outer", 1)
            grad_acc, loss_acc = passed_along((grad_acc, loss_acc), "outer", 1)
    grad_acc, loss_acc = passed_along((grad_acc, loss_acc), "outer", -REACH)
    return (loss_acc, grad_acc)


def per_device(image_emb, text_emb, log_scale, bias):
    unit_i, inv_i, zi = normalize(image_emb)
    unit_t, inv_t, zt = normalize(text_emb)
    scale = jnp.exp(log_scale[0])
    offset = bias[0]
    texts = lax.all_gather(zt, "inner", axis=0, tiled=True)
    images = lax.all_gather(zi, "inner", axis=0, tiled=True)
    local_n = zi.shape[0]
    inner_pos = lax.axis_index("inner")
    columns = jnp.arange(texts.shape[0], dtype=jnp.int32)[None, :]
    target = inner_pos * local_n + jnp.arange(local_n, dtype=jnp.int32)[:, None]
    matches = columns == target
    loss_own, grad_own = cycle_pass(zi, texts, matches, scale, offset)
    unused, text_own = cycle_pass(zt, images, matches, scale, offset)
    grad_image = backprop(unit_i, inv_i, grad_own)
    grad_text = backprop(unit_t, inv_t, text_own)
    return (loss_own, grad_image, grad_text)


def solution(mesh):
    in_specs = (P(("outer", "inner"), None), P(("outer", "inner"), None), P(), P())
    out_specs = (P(("outer", "inner")), P(("outer", "inner"), None), P(("outer", "inner"), None))
    return jax.shard_map(
        per_device, mesh=mesh, in_specs=in_specs, out_specs=out_specs, check_vma=False
    )
```

profile of v0, /device:TPU:6, one launch (start us, length us, event | category | flops | bytes accessed | tf_op | source)
XLA Modules:
  0.0 298.3 jit_solution(14778135614543208828)
XLA Ops:
  7.2 0.0 all-gather.5.cloned.1.call-start
  7.2 1.1 fusion.41
  8.3 1.8 fusion.37
  10.1 0.0 all-gather.5.cloned.1.call-update
  10.1 0.0 all-gather.3.cloned.1.call-start
  10.2 1.1 fusion.45
  11.3 1.8 fusion.34
  13.1 10.8 %collective-permute-start.9 = (bf16[128,1152]{1,0:T(8,128)(2,1)}, bf16[128,1152]{1,0:T(8,128)(2,1)S(1)}, u32[]{:S(2)}, u32[]{:S(2)}) collective-permute-start(bf16[128,1152]{1,0:T(8,128)(2,1)} %fusion.34), channel_id=1, source_target_pairs={{0,496},{16,0},{32,16},{48,32},{64,48},{80,64},{96,80},{112,96},{1... | collective-permute-start | bytes 884744 | tf_op jit(solution)/shard_map/ppermute | solution.py:14
  23.9 1.9 collective-permute-start
  25.9 5.8 %collective-permute-done.9 = bf16[128,1152]{1,0:T(8,128)(2,1)S(1)} collective-permute-done((bf16[128,1152]{1,0:T(8,128)(2,1)}, bf16[128,1152]{1,0:T(8,128)(2,1)S(1)}, u32[]{:S(2)}, u32[]{:S(2)}) %collective-permute-start.9) | collective-permute-done | bytes 294944 | tf_op jit(solution)/shard_map/ppermute | solution.py:14
  31.6 1.9 collective-permute-start.11
  33.6 3.3 %collective-permute-done = bf16[128,1152]{1,0:T(8,128)(2,1)S(1)} collective-permute-done((bf16[128,1152]{1,0:T(8,128)(2,1)}, bf16[128,1152]{1,0:T(8,128)(2,1)S(1)}, u32[]{:S(2)}, u32[]{:S(2)}) %collective-permute-start) | collective-permute-done | bytes 294944 | tf_op jit(solution)/shard_map/ppermute | solution.py:14
  36.9 1.9 collective-permute-start.2
  40.1 0.5 iota_add_fusion
  40.6 8.7 %collective-permute-done.11 = bf16[128,1152]{1,0:T(8,128)(2,1)S(1)} collective-permute-done((bf16[128,1152]{1,0:T(8,128)(2,1)S(1)}, bf16[128,1152]{1,0:T(8,128)(2,1)S(1)}, u32[]{:S(2)}, u32[]{:S(2)}) %collective-permute-start.11) | collective-permute-done | bytes 294944 | tf_op jit(solution)/shard_map/ppermute | solution.py:14
  49.3 1.9 collective-permute-start.13
  51.2 3.2 %collective-permute-done.2 = bf16[128,1152]{1,0:T(8,128)(2,1)S(1)} collective-permute-done((bf16[128,1152]{1,0:T(8,128)(2,1)S(1)}, bf16[128,1152]{1,0:T(8,128)(2,1)S(1)}, u32[]{:S(2)}, u32[]{:S(2)}) %collective-permute-start.2) | collective-permute-done | bytes 294944 | tf_op jit(solution)/shard_map/ppermute | solution.py:14
  54.4 3.7 %collective-permute-start.4 = (bf16[128,1152]{1,0:T(8,128)(2,1)S(1)}, bf16[128,1152]{1,0:T(8,128)(2,1)S(1)}, u32[]{:S(2)}, u32[]{:S(2)}) collective-permute-start(bf16[128,1152]{1,0:T(8,128)(2,1)S(1)} %collective-permute-done.2), channel_id=1, source_target_pairs={{0,16},{16,32},{32,48},{48,64},{64,80},{80,96},{96,112},{112,128},... | collective-permute-start | bytes 884744 | tf_op jit(solution)/shard_map/ppermute | solution.py:14
  58.2 56.2 %all-gather.5.cloned.1.call-done = bf16[2048,1152]{1,0:T(8,128)(2,1)} async-done(((bf16[128,1152]{1,0:T(8,128)(2,1)}), bf16[2048,1152]{1,0:T(8,128)(2,1)}) %all-gather.5.cloned.1.call-update) | async-done | bytes 4718608 | tf_op jit(solution)/shard_map/all_gather | solution.py:66
  114.4 6.1 %convolution_multiply_fusion.2 = f32[128,1152]{1,0:T(8,128)S(1)} fusion(bf16[2048,1152]{1,0:T(8,128)(2,1)} %all-gather.5.cloned.1.call-done, bf16[128,1152]{1,0:T(8,128)(2,1)S(1)} %collective-permute-done.9, f32[]{:T(128)} %bitcast.23, f32[]{:T(128)} %bitcast), kind=kOutput, calls=%fused_computation.6 | convolution fusion | flops 1209679872 | bytes 5603336 | tf_op jit(solution)/shard_map/dot_general | solution.py:32
  120.5 1.9 collective-permute-start.10
  122.4 85.3 %all-gather.3.cloned.1.call-done = bf16[2048,1152]{1,0:T(8,128)(2,1)} async-done(((bf16[128,1152]{1,0:T(8,128)(2,1)}), bf16[2048,1152]{1,0:T(8,128)(2,1)}) %all-gather.3.cloned.1.call-update) | async-done | bytes 4718608 | tf_op jit(solution)/shard_map/all_gather | solution.py:65
  207.7 4.5 %fusion.28 = (f32[128]{0:T(128)S(1)}, f32[128,2048]{1,0:T(8,128)S(1)}) fusion(f32[]{:T(128)} %bitcast.20, bf16[128,1152]{1,0:T(8,128)(2,1)S(1)} %collective-permute-done, bf16[2048,1152]{1,0:T(8,128)(2,1)} %all-gather.3.cloned.1.call-done, f32[]{:T(128)} %bitcast), kind=kOutput, calls=%fused_computation.46 | convolution fusion | flops 606338944 | bytes 6062600 | tf_op jit(solution)/shard_map/dot_general | solution.py:25
  212.2 0.9 convolution_multiply_fusion.5
  213.1 1.9 collective-permute-start.6
  215.1 2.9 collective-permute-start.1
  218.0 6.2 %fusion = f32[128,1152]{1,0:T(8,128)S(1)} fusion(f32[128,1152]{1,0:T(8,128)S(1)} %collective-permute-done.10, bf16[2048,1152]{1,0:T(8,128)(2,1)} %all-gather.5.cloned.1.call-done, bf16[128,1152]{1,0:T(8,128)(2,1)S(1)} %collective-permute-done.11, s32[128]{0:T(128)} %iota_add_fusion, f32[]{:T(128)} %bitcast.22, f32[]{:T(128)} %bitcast), kind=kOutput, calls=%fused_computation.5 | convolution fusion | flops 1210613760 | bytes 6193672 | tf_op jit(solution)/shard_map/dot_general | solution.py:32
  224.1 3.3 %collective-permute-start.12 = (f32[128,1152]{1,0:T(8,128)S(1)}, f32[128,1152]{1,0:T(8,128)S(1)}, u32[]{:S(2)}, u32[]{:S(2)}) collective-permute-start(f32[128,1152]{1,0:T(8,128)S(1)} %fusion), channel_id=1, source_target_pairs={{0,16},{16,32},{32,48},{48,64},{64,80},{80,96},{96,112},{112,128},... | collective-permute-start | bytes 1769480 | tf_op jit(solution)/shard_map/ppermute | solution.py:14
  227.4 4.5 %fusion.29 = (f32[128]{0:T(128)S(1)}, f32[128,2048]{1,0:T(8,128)S(1)}) fusion(s32[128]{0:T(128)} %iota_add_fusion, f32[]{:T(128)} %bitcast.25, bf16[128,1152]{1,0:T(8,128)(2,1)S(1)} %collective-permute-done.2, bf16[2048,1152]{1,0:T(8,128)(2,1)} %all-gather.3.cloned.1.call-done, f32[]{:T(128)} %bitcast), kind=kOutput, calls=%fused_computation.47 | convolution fusion | flops 607387520 | bytes 6063112 | tf_op jit(solution)/shard_map/dot_general | solution.py:25
  231.9 3.2 %collective-permute-done.1 = f32[128]{0:T(128)S(1)} collective-permute-done((f32[128]{0:T(128)S(1)}, f32[128]{0:T(128)S(1)}, u32[]{:S(2)}, u32[]{:S(2)}) %collective-permute-start.1) | collective-permute-done | bytes 544 | tf_op jit(solution)/shard_map/ppermute | solution.py:14
  235.2 2.5 collective-permute-start.3
  237.7 1.0 fusion.1
  238.8 1.9 collective-permute-start.7
  240.7 7.0 %collective-permute-done.12 = f32[128,1152]{1,0:T(8,128)S(1)} collective-permute-done((f32[128,1152]{1,0:T(8,128)S(1)}, f32[128,1152]{1,0:T(8,128)S(1)}, u32[]{:S(2)}, u32[]{:S(2)}) %collective-permute-start.12) | collective-permute-done | bytes 589856 | tf_op jit(solution)/shard_map/ppermute | solution.py:14
  247.7 6.2 %fusion.31 = f32[128,1152]{1,0:T(8,128)S(1)} fusion(f32[128,1152]{1,0:T(8,128)S(1)} %collective-permute-done.12, bf16[2048,1152]{1,0:T(8,128)(2,1)} %all-gather.5.cloned.1.call-done, bf16[128,1152]{1,0:T(8,128)(2,1)S(1)} %collective-permute-done.13, f32[]{:T(128)} %bitcast.21, f32[]{:T(128)} %bitcast), kind=kOutput, calls=%fused_computation.52 | convolution fusion | flops 1209827328 | bytes 6193160 | tf_op jit(solution)/shard_map/dot_general | solution.py:32
  253.9 2.1 collective-permute-start.14
  256.0 4.3 %fusion.30 = (f32[128]{0:T(128)S(1)}, f32[128,2048]{1,0:T(8,128)S(1)}) fusion(f32[]{:T(128)} %bitcast.24, bf16[128,1152]{1,0:T(8,128)(2,1)S(1)} %collective-permute-done.4, bf16[2048,1152]{1,0:T(8,128)(2,1)} %all-gather.3.cloned.1.call-done, f32[]{:T(128)} %bitcast), kind=kOutput, calls=%fused_computation.48 | convolution fusion | flops 606338944 | bytes 6062600 | tf_op jit(solution)/shard_map/dot_general | solution.py:25
  260.4 3.7 %collective-permute-start.5 = (f32[128]{0:T(128)S(1)}, f32[128]{0:T(128)S(1)}, u32[]{:S(2)}, u32[]{:S(2)}) collective-permute-start(f32[128]{0:T(128)S(1)} %add.111), channel_id=1, source_target_pairs={{0,496},{16,0},{32,16},{48,32},{64,48},{80,64},{96,80},{112,96},{1... | collective-permute-start | bytes 1544 | tf_op jit(solution)/shard_map/ppermute | solution.py:14
  264.1 3.4 %convolution_multiply_fusion.3 = f32[128,1152]{1,0:T(8,128)S(1)} fusion(bf16[2048,1152]{1,0:T(8,128)(2,1)} %all-gather.3.cloned.1.call-done, f32[128,2048]{1,0:T(8,128)S(1)} %get-tuple-element.8, f32[]{:T(128)} %bitcast), kind=kOutput, calls=%fused_computation.7 | convolution fusion | flops 605175808 | bytes 6356996 | tf_op jit(solution)/shard_map/dot_general | solution.py:32
  267.5 5.1 %collective-permute-done.5 = f32[128]{0:T(128)S(1)} collective-permute-done((f32[128]{0:T(128)S(1)}, f32[128]{0:T(128)S(1)}, u32[]{:S(2)}, u32[]{:S(2)}) %collective-permute-start.5) | collective-permute-done | bytes 544 | tf_op jit(solution)/shard_map/ppermute | solution.py:14
  272.6 0.1 add.116
  272.6 3.4 %collective-permute-start.8 = (f32[128,1152]{1,0:T(8,128)S(1)}, f32[128,1152]{1,0:T(8,128)S(1)}, u32[]{:S(2)}, u32[]{:S(2)}) collective-permute-start(f32[128,1152]{1,0:T(8,128)S(1)} %add.116), channel_id=1, source_target_pairs={{0,496},{16,0},{32,16},{48,32},{64,48},{80,64},{96,80},{112,96},{1... | collective-permute-start | bytes 1769480 | tf_op jit(solution)/shard_map/ppermute | solution.py:14
  276.0 0.2 fusion.42
  276.3 1.0 fusion.44
  277.3 12.4 %collective-permute-done.8 = f32[128,1152]{1,0:T(8,128)S(1)} collective-permute-done((f32[128,1152]{1,0:T(8,128)S(1)}, f32[128,1152]{1,0:T(8,128)S(1)}, u32[]{:S(2)}, u32[]{:S(2)}) %collective-permute-start.8) | collective-permute-done | bytes 589856 | tf_op jit(solution)/shard_map/ppermute | solution.py:14
  289.7 0.2 fusion.38
  290.0 1.0 fusion.40
  291.0 0.5 copy.10
  (25 shorter events, 0.1 us)
Async XLA Ops:
  7.2 107.2 %all-gather.5.cloned.1.call-start = ((), (), s32[]{:S(2)}) async-start(), calls=%async_computation.1 | async-start | bytes 5013504 | tf_op jit(solution)/shard_map/all_gather | solution.py:66
  10.1 197.6 %all-gather.3.cloned.1.call-start = ((), (), s32[]{:S(2)}) async-start(), calls=%async_computation | async-start | bytes 5013504 | tf_op jit(solution)/shard_map/all_gather | solution.py:65
  13.1 18.5 %collective-permute-start.9 = (bf16[128,1152]{1,0:T(8,128)(2,1)}, bf16[128,1152]{1,0:T(8,128)(2,1)S(1)}, u32[]{:S(2)}, u32[]{:S(2)}) collective-permute-start(bf16[128,1152]{1,0:T(8,128)(2,1)} %fusion.34), channel_id=1, source_target_pairs={{0,496},{16,0},{32,16},{48,32},{64,48},{80,64},{96,80},{112,96},{1... | collective-permute-start | bytes 884744 | tf_op jit(solution)/shard_map/ppermute | solution.py:14
  23.9 12.9 %collective-permute-start = (bf16[128,1152]{1,0:T(8,128)(2,1)}, bf16[128,1152]{1,0:T(8,128)(2,1)S(1)}, u32[]{:S(2)}, u32[]{:S(2)}) collective-permute-start(bf16[128,1152]{1,0:T(8,128)(2,1)} %fusion.37), channel_id=1, source_target_pairs={{0,496},{16,0},{32,16},{48,32},{64,48},{80,64},{96,80},{112,96},{1... | collective-permute-start | bytes 884744 | tf_op jit(solution)/shard_map/ppermute | solution.py:14
  31.6 17.7 %collective-permute-start.11 = (bf16[128,1152]{1,0:T(8,128)(2,1)S(1)}, bf16[128,1152]{1,0:T(8,128)(2,1)S(1)}, u32[]{:S(2)}, u32[]{:S(2)}) collective-permute-start(bf16[128,1152]{1,0:T(8,128)(2,1)S(1)} %collective-permute-done.9), channel_id=1, source_target_pairs={{0,16},{16,32},{32,48},{48,64},{64,80},{80,96},{96,112},{112,128},... | collective-permute-start | bytes 884744 | tf_op jit(solution)/shard_map/ppermute | solution.py:14
  36.9 17.6 %collective-permute-start.2 = (bf16[128,1152]{1,0:T(8,128)(2,1)S(1)}, bf16[128,1152]{1,0:T(8,128)(2,1)S(1)}, u32[]{:S(2)}, u32[]{:S(2)}) collective-permute-start(bf16[128,1152]{1,0:T(8,128)(2,1)S(1)} %collective-permute-done), channel_id=1, source_target_pairs={{0,16},{16,32},{32,48},{48,64},{64,80},{80,96},{96,112},{112,128},... | collective-permute-start | bytes 884744 | tf_op jit(solution)/shard_map/ppermute | solution.py:14
  49.3 191.4 %collective-permute-start.13 = (bf16[128,1152]{1,0:T(8,128)(2,1)S(1)}, bf16[128,1152]{1,0:T(8,128)(2,1)S(1)}, u32[]{:S(2)}, u32[]{:S(2)}) collective-permute-start(bf16[128,1152]{1,0:T(8,128)(2,1)S(1)} %collective-permute-done.11), channel_id=1, source_target_pairs={{0,16},{16,32},{32,48},{48,64},{64,80},{80,96},{96,112},{112,128},... | collective-permute-start | bytes 884744 | tf_op jit(solution)/shard_map/ppermute | solution.py:14
  54.4 201.6 %collective-permute-start.4 = (bf16[128,1152]{1,0:T(8,128)(2,1)S(1)}, bf16[128,1152]{1,0:T(8,128)(2,1)S(1)}, u32[]{:S(2)}, u32[]{:S(2)}) collective-permute-start(bf16[128,1152]{1,0:T(8,128)(2,1)S(1)} %collective-permute-done.2), channel_id=1, source_target_pairs={{0,16},{16,32},{32,48},{48,64},{64,80},{80,96},{96,112},{112,128},... | collective-permute-start | bytes 884744 | tf_op jit(solution)/shard_map/ppermute | solution.py:14
  120.5 97.4 %collective-permute-start.10 = (f32[128,1152]{1,0:T(8,128)S(1)}, f32[128,1152]{1,0:T(8,128)S(1)}, u32[]{:S(2)}, u32[]{:S(2)}) collective-permute-start(f32[128,1152]{1,0:T(8,128)S(1)} %convolution_multiply_fusion.2), channel_id=1, source_target_pairs={{0,16},{16,32},{32,48},{48,64},{64,80},{80,96},{96,112},{112,128},... | collective-permute-start | bytes 1769480 | tf_op jit(solution)/shard_map/ppermute | solution.py:14
  207.7 4.5 %copy-start.2 = (bf16[2048,1152]{1,0:T(8,128)(2,1)S(1)}, bf16[2048,1152]{1,0:T(8,128)(2,1)}, u32[]{:S(2)}) copy-start(bf16[2048,1152]{1,0:T(8,128)(2,1)} %all-gather.3.cloned.1.call-done) | copy-start | bytes 14155780
  213.1 24.5 %collective-permute-start.6 = (f32[128,1152]{1,0:T(8,128)S(1)}, f32[128,1152]{1,0:T(8,128)S(1)}, u32[]{:S(2)}, u32[]{:S(2)}) collective-permute-start(f32[128,1152]{1,0:T(8,128)S(1)} %convolution_multiply_fusion.5), channel_id=1, source_target_pairs={{0,16},{16,32},{32,48},{48,64},{64,80},{80,96},{96,112},{112,128},... | collective-permute-start | bytes 1769480 | tf_op jit(solution)/shard_map/ppermute | solution.py:14
  215.1 20.1 %collective-permute-start.1 = (f32[128]{0:T(128)S(1)}, f32[128]{0:T(128)S(1)}, u32[]{:S(2)}, u32[]{:S(2)}) collective-permute-start(f32[128]{0:T(128)S(1)} %get-tuple-element.3), channel_id=1, source_target_pairs={{0,16},{16,32},{32,48},{48,64},{64,80},{80,96},{96,112},{112,128},... | collective-permute-start | bytes 1544 | tf_op jit(solution)/shard_map/ppermute | solution.py:14
  224.1 13.6 %slice-start = ((s8[4718592]{0:T(1024)(128)(4,1)}), s8[4194304]{0:T(1024)(128)(4,1)S(1)}, s32[]{:S(2)}) async-start(s8[4718592]{0:T(1024)(128)(4,1)} %bitcast.26), calls=%async_computation.2 | async-start | bytes 8388608
  224.1 13.6 %copy-start.3 = (s32[128]{0:T(128)S(1)}, s32[128]{0:T(128)}, u32[]{:S(2)}) copy-start(s32[128]{0:T(128)} %iota_add_fusion) | copy-start | bytes 1540
  224.1 23.6 %collective-permute-start.12 = (f32[128,1152]{1,0:T(8,128)S(1)}, f32[128,1152]{1,0:T(8,128)S(1)}, u32[]{:S(2)}, u32[]{:S(2)}) collective-permute-start(f32[128,1152]{1,0:T(8,128)S(1)} %fusion), channel_id=1, source_target_pairs={{0,16},{16,32},{32,48},{48,64},{64,80},{80,96},{96,112},{112,128},... | collective-permute-start | bytes 1769480 | tf_op jit(solution)/shard_map/ppermute | solution.py:14
  227.4 10.3 %slice-start.1 = ((s8[4718592]{0:T(1024)(128)(4,1)}), s8[524288]{0:T(1024)(128)(4,1)S(1)}, s32[]{:S(2)}) async-start(s8[4718592]{0:T(1024)(128)(4,1)} %bitcast.26), calls=%async_computation.3 | async-start | bytes 1048576
  235.2 25.2 %collective-permute-start.3 = (f32[128]{0:T(128)S(1)}, f32[128]{0:T(128)S(1)}, u32[]{:S(2)}, u32[]{:S(2)}) collective-permute-start(f32[128]{0:T(128)S(1)} %add.108), channel_id=1, source_target_pairs={{0,16},{16,32},{32,48},{48,64},{64,80},{80,96},{96,112},{112,128},... | collective-permute-start | bytes 1544 | tf_op jit(solution)/shard_map/ppermute | solution.py:14
  238.8 33.8 %collective-permute-start.7 = (f32[128,1152]{1,0:T(8,128)S(1)}, f32[128,1152]{1,0:T(8,128)S(1)}, u32[]{:S(2)}, u32[]{:S(2)}) collective-permute-start(f32[128,1152]{1,0:T(8,128)S(1)} %fusion.1), channel_id=1, source_target_pairs={{0,16},{16,32},{32,48},{48,64},{64,80},{80,96},{96,112},{112,128},... | collective-permute-start | bytes 1769480 | tf_op jit(solution)/shard_map/ppermute | solution.py:14
  253.9 22.1 %collective-permute-start.14 = (f32[128,1152]{1,0:T(8,128)S(1)}, f32[128,1152]{1,0:T(8,128)S(1)}, u32[]{:S(2)}, u32[]{:S(2)}) collective-permute-start(f32[128,1152]{1,0:T(8,128)S(1)} %fusion.31), channel_id=1, source_target_pairs={{0,496},{16,0},{32,16},{48,32},{64,48},{80,64},{96,80},{112,96},{1... | collective-permute-start | bytes 1769480 | tf_op jit(solution)/shard_map/ppermute | solution.py:14
  260.4 12.2 %collective-permute-start.5 = (f32[128]{0:T(128)S(1)}, f32[128]{0:T(128)S(1)}, u32[]{:S(2)}, u32[]{:S(2)}) collective-permute-start(f32[128]{0:T(128)S(1)} %add.111), channel_id=1, source_target_pairs={{0,496},{16,0},{32,16},{48,32},{64,48},{80,64},{96,80},{112,96},{1... | collective-permute-start | bytes 1544 | tf_op jit(solution)/shard_map/ppermute | solution.py:14
  264.1 12.0 %copy-start = (bf16[128,1152]{1,0:T(8,128)(2,1)S(1)}, bf16[128,1152]{1,0:T(8,128)(2,1)}, u32[]{:S(2)}) copy-start(bf16[128,1152]{1,0:T(8,128)(2,1)} %param.5) | copy-start | bytes 884740
  264.1 25.6 %copy-start.1 = (bf16[128,1152]{1,0:T(8,128)(2,1)S(1)}, bf16[128,1152]{1,0:T(8,128)(2,1)}, u32[]{:S(2)}) copy-start(bf16[128,1152]{1,0:T(8,128)(2,1)} %param.4) | copy-start | bytes 884740
  272.6 17.1 %collective-permute-start.8 = (f32[128,1152]{1,0:T(8,128)S(1)}, f32[128,1152]{1,0:T(8,128)S(1)}, u32[]{:S(2)}, u32[]{:S(2)}) collective-permute-start(f32[128,1152]{1,0:T(8,128)S(1)} %add.116), channel_id=1, source_target_pairs={{0,496},{16,0},{32,16},{48,32},{64,48},{80,64},{96,80},{112,96},{1... | collective-permute-start | bytes 1769480 | tf_op jit(solution)/shard_map/ppermute | solution.py:14
Sparse Core Ops, SparseCore 0:
  11.8 102.5 all-gather.4
  118.2 89.4 all-gather.2
where the time goes:
time: 299 us; the launch traced here: 298 us
  waiting for transfers between devices  190 us (64%)
  starting transfers between devices  45.8 us (15%)
  matrix products  37.1 us (12%)
  between operations  15.7 us (5%)
  other arithmetic  8.94 us (3%)
    all_gather x1, waiting for transfers between devices, per_device(): texts = lax.all_gather(zt, 'inner', axis=0, tiled=True)  85.3 us
    all_gather x1, waiting for transfers between devices, per_device(): images = lax.all_gather(zi, 'inner', axis=0, tiled=True)  56.2 us
    ppermute x15, waiting for transfers between devices, passed_along(): lax.ppermute(value, axis, [(i, (i + by) % length) for i in range(length)])  48.8 us
    ppermute x15, starting transfers between devices, passed_along(): lax.ppermute(value, axis, [(i, (i + by) % length) for i in range(length)])  45.8 us
    dot_general x6, matrix products, tile_terms(): jnp.dot(weights, partners, preferred_element_type=jnp.float32)  23.7 us
    dot_general x3, matrix products, tile_terms(): lax.dot_general(block, partners, (((1,), (1,)), ((), ())), preferred_elem...  13.3 us
  transfers between devices with their start and end apart: 17, of which 10 were waited for; matrix products, arithmetic and copies ran while one was open for 14% of the time, Pallas kernels for 0%

commit v1 on v0

v1 whole, which is shorter than its diff:
```python
import jax
import jax.numpy as jnp
from jax import lax
from jax.experimental import pallas as pl
from jax.experimental.pallas import tpu as pltpu
from jax.sharding import PartitionSpec as P

MESH = pl.DeviceIdType.MESH
EPS = 1e-06

X_N = 4
Z_LO = 4
Z_N = 8

OWN, FAR, PREV, NEXT = 0, 1, 2, 3


def unit_of(raw):
    wide = raw.astype(jnp.float32)
    inverse = lax.rsqrt(jnp.sum(wide * wide, axis=1, keepdims=True) + EPS)
    return wide * inverse, inverse


def places(groups):
    outer = lax.axis_index("outer")
    inner = lax.axis_index("inner")
    y, z_lo = outer // Z_LO, outer % Z_LO
    x, z_hi, core = inner // 4, (inner // 2) % 2, inner % 2

    def inner_of(x, z_hi, core):
        return x * 4 + z_hi * 2 + core

    def along_z(by):
        z = (z_hi * Z_LO + z_lo + by + Z_N) % Z_N
        return (y * Z_LO + z % Z_LO, inner_of(x, z // Z_LO, core))

    last = (z_lo == Z_LO - 1).astype(jnp.int32)
    first = (z_lo == 0).astype(jnp.int32)
    return {
        "xn": (outer, inner_of((x + 1) % X_N, z_hi, core)),
        "xp": (outer, inner_of((x + X_N - 1) % X_N, z_hi, core)),
        "zn": along_z(2),
        "zp": along_z(-2),
        "sib": (outer, inner_of(x, z_hi, 1 - core)),
        "gn": ((outer + 1) % groups, inner_of(x, (z_hi + last) % 2, core)),
        "gp": ((outer + groups - 1) % groups, inner_of(x, (z_hi + first) % 2, core)),
    }


def kernel(
    groups, ls_ref, b_ref, img_ref, txt_ref, loss_ref, gi_ref, gt_ref,
    texts, images, wt, tg, ig, loss_acc, relay, far_s, far_r, row_s, row_r, col_s, back, col_r,
    sib_s, sib_r, sib_ls, sib_lr, ret_s, ret_r, ret_ls, ret_lr, ssem, rsem,
):
    rows, width = img_ref.shape
    half = rows // 2
    pair = 2 * rows
    tile = width // 3 if width % 384 == 0 else width
    halves = (pl.ds(0, half), pl.ds(half, half))
    peers = places(groups)
    messages = []

    def message(src, dst, peer):
        index = len(messages)
        messages.append(
            pltpu.make_async_remote_copy(
                src_ref=src, dst_ref=dst, send_sem=ssem.at[index], recv_sem=rsem.at[index],
                device_id=peers[peer], device_id_type=MESH,
            )
        )
        return messages[-1]

    def slot(r, k):
        return (r * 4 + k) * rows

    def text(r, k, h):
        return texts.at[pl.ds(slot(r, k) + h * half, half), :]

    def image(k):
        return images.at[pl.ds(k * rows, rows), :]

    z_out = [message(text(0, OWN, 0), relay.at[halves[0], :], "zn"), message(text(0, OWN, 1), relay.at[halves[1], :], "zp")]
    z_on = [message(relay.at[halves[0], :], text(1, OWN, 0), "zn"), message(relay.at[halves[1], :], text(1, OWN, 1), "zp")]
    to_next = [[message(text(r, OWN, h), text(r, PREV, h), "xn") for h in range(2)] for r in range(2)]
    to_prev = [[message(text(r, OWN, h), text(r, NEXT, h), "xp") for h in range(2)] for r in range(2)]
    far_on = [
        [message(text(r, PREV, 0), text(r, FAR, 0), "xn"), message(text(r, NEXT, 1), text(r, FAR, 1), "xp")]
        for r in range(2)
    ]
    img_next = message(image(0), image(1), "gn")
    img_prev = message(image(0), image(2), "gp")
    img_sib = [message(image(k), image(3 + k), "sib") for k in range(3)]
    far_back = [
        [message(far_s.at[r, halves[h], :], far_r.at[r, halves[h], :], "xp" if h == 0 else "xn") for h in range(2)]
        for r in range(2)
    ]
    row_back = [
        [[message(row_s.at[r, s, halves[h], :], row_r.at[r, s, halves[h], :], "xp" if s == 0 else "xn") for h in range(2)]
         for s in range(2)]
        for r in range(2)
    ]
    z_back = [message(col_s.at[halves[h], :], back.at[halves[h], :], "zp" if h == 0 else "zn") for h in range(2)]
    z_home = [message(back.at[halves[h], :], col_r.at[halves[h], :], "zp" if h == 0 else "zn") for h in range(2)]
    sib_back = [message(sib_s.at[k], sib_r.at[k], "sib") for k in range(3)]
    sib_loss = message(sib_ls, sib_lr, "sib")
    ret = [message(ret_s.at[0], ret_r.at[1], "gp"), message(ret_s.at[1], ret_r.at[0], "gn")]
    ret_loss = [message(ret_ls.at[0], ret_lr.at[1], "gp"), message(ret_ls.at[1], ret_lr.at[0], "gn")]

    barrier = pltpu.get_barrier_semaphore()
    for peer in peers.values():
        pl.semaphore_signal(barrier, inc=1, device_id=peer, device_id_type=MESH)

    texts[pl.ds(0, rows), :] = unit_of(txt_ref[...])[0].astype(jnp.bfloat16)
    images[pl.ds(0, rows), :] = unit_of(img_ref[...])[0].astype(jnp.bfloat16)
    loss_acc[...] = jnp.zeros_like(loss_acc)
    scale = jnp.exp(jnp.full((1, pair), ls_ref[0], jnp.float32))
    offset = b_ref[0]
    pl.semaphore_wait(barrier, len(peers))

    for h in range(2):
        z_out[h].start()
    to_next[0][0].start()
    to_prev[0][1].start()
    img_next.start()
    img_prev.start()
    img_sib[0].start()
    to_next[0][1].start()
    to_prev[0][0].start()

    def weigh(start, j, diagonal):
        columns = pl.ds(pl.multiple_of(j * pair, pair), pair)
        dots = lax.dot_general(
            texts[pl.ds(start, pair), :], images[columns, :], (((1,), (1,)), ((), ())),
            preferred_element_type=jnp.float32,
        )
        logits = scale * dots + offset
        grown = jnp.exp(logits)
        whole = 1.0 + grown
        weights = grown / whole
        if diagonal:
            row = lax.broadcasted_iota(jnp.int32, (pair, pair), 0)
            column = lax.broadcasted_iota(jnp.int32, (pair, pair), 1)
            positive = (row == column) & (row < rows)
            weights = weights - positive.astype(jnp.float32)
            whole = jnp.where(positive, 1.0 + jnp.exp(-logits), whole)
        wt[pl.ds(start, pair), columns] = weights.astype(jnp.bfloat16)
        q = pair // 4
        product = (whole[:q] * whole[q:2 * q]) * (whole[2 * q:3 * q] * whole[3 * q:])
        loss_acc[j] += jnp.sum(jnp.log(product).reshape(q // 8, 8, pair), axis=0)

    def text_partial(start):
        def step(n, carry):
            columns = pl.ds(pl.multiple_of(n * tile, 128), tile)
            tg[pl.ds(start, pair), columns] = jnp.dot(
                wt[pl.ds(start, pair), :], images[:, columns], preferred_element_type=jnp.float32
            )
            return carry
        lax.fori_loop(0, width // tile, step, 0)

    def both(start, diagonal):
        def step(j, carry):
            weigh(start, j, False)
            return carry
        if diagonal:
            weigh(start, 0, True)
        lax.fori_loop(1 if diagonal else 0, 3, step, 0)
        text_partial(start)

    def image_partial(first):
        def step(n, carry):
            columns = pl.ds(pl.multiple_of(n * tile, 128), tile)
            ig[pl.ds(first, 3 * rows), columns] = lax.dot_general(
                wt[:, pl.ds(first, 3 * rows)], texts[:, columns], (((0,), (0,)), ((), ())),
                preferred_element_type=jnp.float32,
            )
            return carry
        lax.fori_loop(0, width // tile, step, 0)

    def partial(r, k, h):
        return tg[pl.ds(slot(r, k) + h * half, half), :]

    def reduce_begin(r):
        far_s[r] = tg[pl.ds(slot(r, FAR), rows), :].astype(jnp.bfloat16)
        far_back[r][0].start()
        far_back[r][1].start()
        row_s[r, 0, halves[1], :] = partial(r, PREV, 1).astype(jnp.bfloat16)
        row_back[r][0][1].start()
        row_s[r, 1, halves[0], :] = partial(r, NEXT, 0).astype(jnp.bfloat16)
        row_back[r][1][0].start()

    def reduce_middle(r):
        far_back[r][0].wait_recv()
        row_s[r, 0, halves[0], :] = (partial(r, PREV, 0) + far_r[r, halves[0], :].astype(jnp.float32)).astype(jnp.bfloat16)
        row_back[r][0][0].start()
        far_back[r][1].wait_recv()
        row_s[r, 1, halves[1], :] = (partial(r, NEXT, 1) + far_r[r, halves[1], :].astype(jnp.float32)).astype(jnp.bfloat16)
        row_back[r][1][1].start()

    def reduce_end(r, h):
        row_back[r][0][h].wait_recv()
        row_back[r][1][h].wait_recv()
        return (
            partial(r, OWN, h)
            + row_r[r, 0, halves[h], :].astype(jnp.float32)
            + row_r[r, 1, halves[h], :].astype(jnp.float32)
        )

    def loss_of(k):
        block = loss_acc[k // 2]
        return jnp.sum(block[:, (k % 2) * rows:(k % 2 + 1) * rows], axis=0, keepdims=True)

    for h in range(2):
        z_out[h].wait_recv()
        z_on[h].start()
    to_next[0][0].wait_recv()
    far_on[0][0].start()
    to_prev[0][1].wait_recv()
    far_on[0][1].start()
    img_next.wait_recv()
    img_sib[1].start()
    img_prev.wait_recv()
    img_sib[2].start()
    to_next[0][1].wait_recv()
    to_prev[0][0].wait_recv()
    for k in range(3):
        img_sib[k].wait_recv()
    both(slot(0, PREV), False)
    for h in range(2):
        z_on[h].wait_recv()
        if h == 0:
            to_next[1][0].start()
            to_prev[1][0].start()
        else:
            to_prev[1][1].start()
            to_next[1][1].start()
    for h in range(2):
        far_on[0][h].wait_recv()
    both(slot(0, OWN), True)
    to_next[1][0].wait_recv()
    far_on[1][0].start()
    to_prev[1][1].wait_recv()
    far_on[1][1].start()
    to_next[1][1].wait_recv()
    to_prev[1][0].wait_recv()
    both(slot(1, PREV), False)
    for h in range(2):
        far_on[1][h].wait_recv()
    both(slot(1, OWN), False)

    reduce_begin(1)
    image_partial(3 * rows)
    for k in (1, 2, 0):
        sib_s[k] = ig[pl.ds((3 + k) * rows, rows), :].astype(jnp.bfloat16)
        sib_back[k].start()
    sib_ls[...] = jnp.zeros_like(sib_ls)
    for k in range(3):
        sib_ls[pl.ds(k, 1), :] = loss_of(3 + k)
    sib_loss.start()
    reduce_middle(1)
    image_partial(0)
    sib_loss.wait_recv()
    for s in range(2):
        sib_back[s + 1].wait_recv()
        ret_s[s] = (ig[pl.ds((s + 1) * rows, rows), :] + sib_r[s + 1].astype(jnp.float32)).astype(jnp.bfloat16)
        ret[s].start()
        ret_ls[s] = jnp.broadcast_to(loss_of(s + 1) + sib_lr[pl.ds(s + 1, 1), :], ret_ls.shape[1:])
        ret_loss[s].start()
    for h in range(2):
        col_s[halves[h], :] = reduce_end(1, h).astype(jnp.bfloat16)
        z_back[h].start()
    reduce_begin(0)
    reduce_middle(0)
    for h in range(2):
        z_back[h].wait_recv()
        z_home[h].start()

    scale_row = jnp.exp(jnp.full((1, width), ls_ref[0], jnp.float32))

    def backprop(raw, grads):
        unit, inverse = unit_of(raw)
        grads = scale_row * grads
        return (grads - unit * jnp.sum(unit * grads, axis=1, keepdims=True)) * inverse

    sib_back[0].wait_recv()
    for s in range(2):
        ret_loss[s].wait_recv()
        ret[s].wait_recv()
    loss_ref[...] = loss_of(0) + sib_lr[pl.ds(0, 1), :] + ret_lr[0, pl.ds(0, 1), :] + ret_lr[1, pl.ds(0, 1), :]
    for h in range(2):
        grads = (
            (ig[pl.ds(h * half, half), :] + sib_r[0, halves[h], :].astype(jnp.float32))
            + (ret_r[0, halves[h], :].astype(jnp.float32) + ret_r[1, halves[h], :].astype(jnp.float32))
        )
        gi_ref[halves[h], :] = backprop(img_ref[halves[h], :], grads)
    for h in range(2):
        near = reduce_end(0, h)
        z_home[h].wait_recv()
        gt_ref[halves[h], :] = backprop(txt_ref[halves[h], :], near + col_r[halves[h], :].astype(jnp.float32))
    for sent in messages:
        sent.wait_send()


N_MESSAGES = 45


def per_device(groups, image_emb, text_emb, log_scale, bias):
    rows, width = image_emb.shape
    half_type, full = jnp.bfloat16, jnp.float32
    vmem = pl.BlockSpec(memory_space=pltpu.VMEM)
    smem = pl.BlockSpec(memory_space=pltpu.SMEM)
    loss, grad_image, grad_text = pl.pallas_call(
        lambda *refs: kernel(groups, *refs),
        out_shape=(
            jax.ShapeDtypeStruct((1, rows), full),
            jax.ShapeDtypeStruct((rows, width), full),
            jax.ShapeDtypeStruct((rows, width), full),
        ),
        in_specs=[smem, smem, vmem, vmem],
        out_specs=(vmem, vmem, vmem),
        scratch_shapes=[
            pltpu.VMEM((8 * rows, width), half_type),
            pltpu.VMEM((6 * rows, width), half_type),
            pltpu.VMEM((8 * rows, 6 * rows), half_type),
            pltpu.VMEM((8 * rows, width), full),
            pltpu.VMEM((6 * rows, width), full),
            pltpu.VMEM((3, 8, 2 * rows), full),
            pltpu.VMEM((rows, width), half_type),
            pltpu.VMEM((2, rows, width), half_type),
            pltpu.VMEM((2, rows, width), half_type),
            pltpu.VMEM((2, 2, rows, width), half_type),
            pltpu.VMEM((2, 2, rows, width), half_type),
            pltpu.VMEM((rows, width), half_type),
            pltpu.VMEM((rows, width), half_type),
            pltpu.VMEM((rows, width), half_type),
            pltpu.VMEM((3, rows, width), half_type),
            pltpu.VMEM((3, rows, width), half_type),
            pltpu.VMEM((8, rows), full),
            pltpu.VMEM((8, rows), full),
            pltpu.VMEM((2, rows, width), half_type),
            pltpu.VMEM((2, rows, width), half_type),
            pltpu.VMEM((2, 8, rows), full),
            pltpu.VMEM((2, 8, rows), full),
            pltpu.SemaphoreType.DMA((N_MESSAGES,)),
            pltpu.SemaphoreType.DMA((N_MESSAGES,)),
        ],
        compiler_params=pltpu.CompilerParams(
            collective_id=0, has_side_effects=True, vmem_limit_bytes=48 * 1024 * 1024
        ),
    )(log_scale, bias, image_emb, text_emb)
    return (loss.reshape(rows), grad_image, grad_text)


def solution(mesh):
    groups = mesh.shape["outer"]
    in_specs = (P(("outer", "inner"), None), P(("outer", "inner"), None), P(), P())
    out_specs = (P(("outer", "inner")), P(("outer", "inner"), None), P(("outer", "inner"), None))
    return jax.shard_map(
        lambda *args: per_device(groups, *args),
        mesh=mesh, in_specs=in_specs, out_specs=out_specs, check_vma=False,
    )
```

time: 299 us -> 87.5 us (0.29)
  the two profiles are of different devices: /device:TPU:6 before, /device:TPU:64 now
where the time goes in v1:
time: 87.5 us; the launch traced here: 87.3 us
  Pallas kernels  81.3 us (93%)
  local copies, waits for them, and re-layouts  4.06 us (5%)
  between operations  1.94 us (2%)
    pallas_call x1, Pallas kernels, per_device(): pl.pallas_call(lambda *refs: kernel(groups, *refs), out_shape=(jax.ShapeD...  81.3 us
    unnamed x7, local copies, waits for them, and re-layouts  4.06 us

profile of v1, /device:TPU:64, one launch (start us, length us, event | category | flops | bytes accessed | tf_op | source)
XLA Modules:
  0.0 87.3 jit_solution(1383902990100424260)
XLA Ops:
  1.9 0.0 copy-start
  1.9 1.0 %copy-done = bf16[128,1152]{1,0:T(8,128)(2,1)S(1)} copy-done((bf16[128,1152]{1,0:T(8,128)(2,1)S(1)}, bf16[128,1152]{1,0:T(8,128)(2,1)}, u32[]{:S(2)}) %copy-start) | copy-done | bytes 294936
  2.9 0.0 copy-start.1
  2.9 1.0 %copy-done.1 = bf16[128,1152]{1,0:T(8,128)(2,1)S(1)} copy-done((bf16[128,1152]{1,0:T(8,128)(2,1)S(1)}, bf16[128,1152]{1,0:T(8,128)(2,1)}, u32[]{:S(2)}) %copy-start.1) | copy-done | bytes 294936
  3.8 81.3 %shard_map.67 = (f32[1,128]{1,0:T(1,128)S(1)}, f32[128,1152]{1,0:T(8,128)S(1)}, f32[128,1152]{1,0:T(8,128)S(1)}) custom-call(f32[1]{0:T(128)S(6)} %copy.10.refs_0_, f32[1]{0:T(128)S(6)} %copy.11.refs_1_, bf16[128,1152]{1,0:T(8,128)(2,1)S(1)} %copy-done, bf16[128,1152]{1,0:T(8,128)(2,1)S(1)} %copy-done.1), custom_call_target="tpu_custom_call" | custom-call | tf_op jit(solution)/shard_map/pallas_call | solution.py:311
  85.1 0.5 copy.12
  85.7 0.8 copy.13
  86.5 0.8 copy.14
Async XLA Ops:
  1.9 1.0 %copy-start = (bf16[128,1152]{1,0:T(8,128)(2,1)S(1)}, bf16[128,1152]{1,0:T(8,128)(2,1)}, u32[]{:S(2)}) copy-start(bf16[128,1152]{1,0:T(8,128)(2,1)} %refs_2_.1) | copy-start | bytes 884740
  2.9 1.0 %copy-start.1 = (bf16[128,1152]{1,0:T(8,128)(2,1)S(1)}, bf16[128,1152]{1,0:T(8,128)(2,1)}, u32[]{:S(2)}) copy-start(bf16[128,1152]{1,0:T(8,128)(2,1)} %refs_3_.1) | copy-start | bytes 884740

commit v2 on v1

v2 whole, which is shorter than its diff:
```python
import jax
import jax.numpy as jnp
from jax import lax
from jax.experimental import pallas as pl
from jax.experimental.pallas import tpu as pltpu
from jax.sharding import PartitionSpec as P

MESH = pl.DeviceIdType.MESH
EPS = 1e-06

X_N = 4
Z_LO = 4
Z_N = 8

OWN, FAR, PREV, NEXT = 0, 1, 2, 3

CHUNKS = 2


def unit_of(raw):
    wide = raw.astype(jnp.float32)
    inverse = lax.rsqrt(jnp.sum(wide * wide, axis=1, keepdims=True) + EPS)
    return wide * inverse, inverse


def places(groups):
    outer = lax.axis_index("outer")
    inner = lax.axis_index("inner")
    y, z_lo = outer // Z_LO, outer % Z_LO
    x, z_hi, core = inner // 4, (inner // 2) % 2, inner % 2

    def inner_of(x, z_hi, core):
        return x * 4 + z_hi * 2 + core

    def along_z(by):
        z = (z_hi * Z_LO + z_lo + by + Z_N) % Z_N
        return (y * Z_LO + z % Z_LO, inner_of(x, z // Z_LO, core))

    last = (z_lo == Z_LO - 1).astype(jnp.int32)
    first = (z_lo == 0).astype(jnp.int32)
    return {
        "xn": (outer, inner_of((x + 1) % X_N, z_hi, core)),
        "xp": (outer, inner_of((x + X_N - 1) % X_N, z_hi, core)),
        "zn": along_z(2),
        "zp": along_z(-2),
        "sib": (outer, inner_of(x, z_hi, 1 - core)),
        "gn": ((outer + 1) % groups, inner_of(x, (z_hi + last) % 2, core)),
        "gp": ((outer + groups - 1) % groups, inner_of(x, (z_hi + first) % 2, core)),
    }


def kernel(
    groups, ls_ref, b_ref, img_ref, txt_ref, loss_ref, gi_ref, gt_ref,
    texts, images, wt, tg, ig, loss_acc, relay, far_s, far_r, row_s, row_r, col_s, back, col_r,
    sib_s, sib_r, sib_ls, sib_lr, ret_s, ret_r, ret_ls, ret_lr, ssem, rsem,
):
    rows, width = img_ref.shape
    sub = rows // CHUNKS
    half = sub // 2
    pair = 2 * rows
    unit = 4 * sub
    tile = width // 3 if width % 384 == 0 else width
    peers = places(groups)
    messages = []

    def message(src, dst, peer):
        index = len(messages)
        messages.append(
            pltpu.make_async_remote_copy(
                src_ref=src, dst_ref=dst, send_sem=ssem.at[index], recv_sem=rsem.at[index],
                device_id=peers[peer], device_id_type=MESH,
            )
        )
        return messages[-1]

    def base(r, c):
        return (r * CHUNKS + c) * unit

    def text(r, c, k, h):
        return texts.at[pl.ds(base(r, c) + k * sub + h * half, half), :]

    def piece(c, h):
        return pl.ds(c * sub + h * half, half)

    def image(k):
        return images.at[pl.ds(k * rows, rows), :]

    def each(make):
        return [[make(c, h) for h in range(2)] for c in range(CHUNKS)]

    def each_row(make):
        return [each(lambda c, h: make(r, c, h)) for r in range(2)]

    z_out = each(lambda c, h: message(text(0, c, OWN, h), relay.at[piece(c, h), :], ("zn", "zp")[h]))
    z_on = each(lambda c, h: message(relay.at[piece(c, h), :], text(1, c, OWN, h), ("zn", "zp")[h]))
    to_next = each_row(lambda r, c, h: message(text(r, c, OWN, h), text(r, c, PREV, h), "xn"))
    to_prev = each_row(lambda r, c, h: message(text(r, c, OWN, h), text(r, c, NEXT, h), "xp"))
    far_on = each_row(lambda r, c, h: message(text(r, c, (PREV, NEXT)[h], h), text(r, c, FAR, h), ("xn", "xp")[h]))
    img_next = message(image(0), image(1), "gn")
    img_prev = message(image(0), image(2), "gp")
    img_sib = [message(image(k), image(3 + k), "sib") for k in range(3)]
    far_back = each_row(lambda r, c, h: message(far_s.at[r, piece(c, h), :], far_r.at[r, piece(c, h), :], ("xp", "xn")[h]))
    row_back = [
        each_row(lambda r, c, h: message(row_s.at[r, s, piece(c, h), :], row_r.at[r, s, piece(c, h), :], ("xp", "xn")[s]))
        for s in range(2)
    ]
    z_back = each(lambda c, h: message(col_s.at[piece(c, h), :], back.at[piece(c, h), :], ("zp", "zn")[h]))
    z_home = each(lambda c, h: message(back.at[piece(c, h), :], col_r.at[piece(c, h), :], ("zp", "zn")[h]))
    sib_back = [message(sib_s.at[k], sib_r.at[k], "sib") for k in range(3)]
    sib_loss = message(sib_ls, sib_lr, "sib")
    ret = [message(ret_s.at[0], ret_r.at[1], "gp"), message(ret_s.at[1], ret_r.at[0], "gn")]
    ret_loss = [message(ret_ls.at[0], ret_lr.at[1], "gp"), message(ret_ls.at[1], ret_lr.at[0], "gn")]

    barrier = pltpu.get_barrier_semaphore()
    for peer in peers.values():
        pl.semaphore_signal(barrier, inc=1, device_id=peer, device_id_type=MESH)

    own = unit_of(txt_ref[...])[0].astype(jnp.bfloat16)
    for c in range(CHUNKS):
        texts[pl.ds(base(0, c), sub), :] = own[c * sub:(c + 1) * sub]
    images[pl.ds(0, rows), :] = unit_of(img_ref[...])[0].astype(jnp.bfloat16)
    loss_acc[...] = jnp.zeros_like(loss_acc)
    scale = jnp.exp(jnp.full((1, pair), ls_ref[0], jnp.float32))
    offset = b_ref[0]
    pl.semaphore_wait(barrier, len(peers))

    def start(*pairs):
        for one in pairs:
            for copy in one:
                copy.start()

    def arrive(*pairs):
        for one in pairs:
            for copy in one:
                copy.wait_recv()

    def weigh(c, start, j, diagonal):
        columns = pl.ds(j * pair, pair)
        dots = lax.dot_general(
            texts[pl.ds(start, unit), :], images[columns, :], (((1,), (1,)), ((), ())),
            preferred_element_type=jnp.float32,
        )
        logits = scale * dots + offset
        grown = jnp.exp(logits)
        whole = 1.0 + grown
        weights = grown / whole
        if diagonal:
            row = lax.broadcasted_iota(jnp.int32, (unit, pair), 0)
            column = lax.broadcasted_iota(jnp.int32, (unit, pair), 1)
            positive = (row + c * sub == column) & (row < sub)
            weights = weights - positive.astype(jnp.float32)
            whole = jnp.where(positive, 1.0 + jnp.exp(-logits), whole)
        wt[pl.ds(start, unit), columns] = weights.astype(jnp.bfloat16)
        q = unit // 4
        product = (whole[:q] * whole[q:2 * q]) * (whole[2 * q:3 * q] * whole[3 * q:])
        loss_acc[j] += jnp.sum(jnp.log(product).reshape(q // 8, 8, pair), axis=0)

    def both(r, c):
        begin = base(r, c)
        for j in range(3):
            weigh(c, begin, j, r == 0 and j == 0)
        for n in range(width // tile):
            columns = pl.ds(n * tile, tile)
            tg[pl.ds(begin, unit), columns] = jnp.dot(
                wt[pl.ds(begin, unit), :], images[:, columns], preferred_element_type=jnp.float32
            )

    def image_partial(first):
        for n in range(width // tile):
            columns = pl.ds(n * tile, tile)
            ig[pl.ds(first, 3 * rows), columns] = lax.dot_general(
                wt[:, pl.ds(first, 3 * rows)], texts[:, columns], (((0,), (0,)), ((), ())),
                preferred_element_type=jnp.float32,
            )

    def partial(r, c, k, h):
        return tg[pl.ds(base(r, c) + k * sub + h * half, half), :]

    def reduce_begin(r, c):
        for h in range(2):
            far_s[r, piece(c, h), :] = partial(r, c, FAR, h).astype(jnp.bfloat16)
            far_back[r][c][h].start()
        for s in range(2):
            row_s[r, s, piece(c, 1 - s), :] = partial(r, c, (PREV, NEXT)[s], 1 - s).astype(jnp.bfloat16)
            row_back[s][r][c][1 - s].start()

    def reduce_middle(r, c):
        for s in range(2):
            far_back[r][c][s].wait_recv()
            total = partial(r, c, (PREV, NEXT)[s], s) + far_r[r, piece(c, s), :].astype(jnp.float32)
            row_s[r, s, piece(c, s), :] = total.astype(jnp.bfloat16)
            row_back[s][r][c][s].start()

    def reduce_end(r, c, h):
        row_back[0][r][c][h].wait_recv()
        row_back[1][r][c][h].wait_recv()
        return (
            partial(r, c, OWN, h)
            + row_r[r, 0, piece(c, h), :].astype(jnp.float32)
            + row_r[r, 1, piece(c, h), :].astype(jnp.float32)
        )

    def column_home(c):
        for h in range(2):
            col_s[piece(c, h), :] = reduce_end(1, c, h).astype(jnp.bfloat16)
            z_back[c][h].start()

    def loss_of(k):
        block = loss_acc[k // 2]
        return jnp.sum(block[:, (k % 2) * rows:(k % 2 + 1) * rows], axis=0, keepdims=True)

    def far_forward(r, c):
        to_next[r][c][0].wait_recv()
        far_on[r][c][0].start()
        to_prev[r][c][1].wait_recv()
        far_on[r][c][1].start()

    def all_here(r, c):
        to_next[r][c][1].wait_recv()
        to_prev[r][c][0].wait_recv()
        arrive(far_on[r][c])

    def row_out(r, c):
        for h in range(2):
            to_next[r][c][h].start()
            to_prev[r][c][1 - h].start()

    start(z_out[0])
    img_next.start()
    img_prev.start()
    row_out(0, 0)
    img_sib[0].start()
    row_out(0, 1)
    for h in range(2):
        z_out[0][h].wait_recv()
        z_on[0][h].start()
    far_forward(0, 0)
    img_next.wait_recv()
    img_sib[1].start()
    img_prev.wait_recv()
    img_sib[2].start()
    start(z_out[1])
    far_forward(0, 1)
    arrive(z_on[0])
    row_out(1, 0)
    arrive(img_sib)
    all_here(0, 0)
    both(0, 0)
    for h in range(2):
        z_out[1][h].wait_recv()
        z_on[1][h].start()
    far_forward(1, 0)
    all_here(0, 1)
    both(0, 1)
    arrive(z_on[1])
    row_out(1, 1)
    all_here(1, 0)
    both(1, 0)
    reduce_begin(1, 0)
    far_forward(1, 1)
    reduce_middle(1, 0)
    all_here(1, 1)
    both(1, 1)

    reduce_begin(1, 1)
    column_home(0)
    image_partial(3 * rows)
    for k in (1, 2, 0):
        sib_s[k] = ig[pl.ds((3 + k) * rows, rows), :].astype(jnp.bfloat16)
        sib_back[k].start()
    sib_ls[...] = jnp.zeros_like(sib_ls)
    for k in range(3):
        sib_ls[pl.ds(k, 1), :] = loss_of(3 + k)
    sib_loss.start()
    reduce_middle(1, 1)
    image_partial(0)
    for h in range(2):
        z_back[0][h].wait_recv()
        z_home[0][h].start()
    column_home(1)
    sib_loss.wait_recv()
    for s in range(2):
        sib_back[s + 1].wait_recv()
        ret_s[s] = (ig[pl.ds((s + 1) * rows, rows), :] + sib_r[s + 1].astype(jnp.float32)).astype(jnp.bfloat16)
        ret[s].start()
        ret_ls[s] = jnp.broadcast_to(loss_of(s + 1) + sib_lr[pl.ds(s + 1, 1), :], ret_ls.shape[1:])
        ret_loss[s].start()
    for c in range(CHUNKS):
        reduce_begin(0, c)
    for h in range(2):
        z_back[1][h].wait_recv()
        z_home[1][h].start()
    for c in range(CHUNKS):
        reduce_middle(0, c)

    scale_row = jnp.exp(jnp.full((1, width), ls_ref[0], jnp.float32))

    def backprop(raw, grads):
        unit, inverse = unit_of(raw)
        grads = scale_row * grads
        return (grads - unit * jnp.sum(unit * grads, axis=1, keepdims=True)) * inverse

    def finish_text(c):
        for h in range(2):
            near = reduce_end(0, c, h)
            z_home[c][h].wait_recv()
            gt_ref[piece(c, h), :] = backprop(txt_ref[piece(c, h), :], near + col_r[piece(c, h), :].astype(jnp.float32))

    finish_text(0)
    sib_back[0].wait_recv()
    for s in range(2):
        ret_loss[s].wait_recv()
        ret[s].wait_recv()
    loss_ref[...] = loss_of(0) + sib_lr[pl.ds(0, 1), :] + ret_lr[0, pl.ds(0, 1), :] + ret_lr[1, pl.ds(0, 1), :]
    for c in range(CHUNKS):
        for h in range(2):
            here = piece(c, h)
            grads = (
                (ig[here, :] + sib_r[0, here, :].astype(jnp.float32))
                + (ret_r[0, here, :].astype(jnp.float32) + ret_r[1, here, :].astype(jnp.float32))
            )
            gi_ref[here, :] = backprop(img_ref[here, :], grads)
    finish_text(1)
    for sent in messages:
        sent.wait_send()


N_MESSAGES = 77


def per_device(groups, image_emb, text_emb, log_scale, bias):
    rows, width = image_emb.shape
    half_type, full = jnp.bfloat16, jnp.float32
    vmem = pl.BlockSpec(memory_space=pltpu.VMEM)
    smem = pl.BlockSpec(memory_space=pltpu.SMEM)
    loss, grad_image, grad_text = pl.pallas_call(
        lambda *refs: kernel(groups, *refs),
        out_shape=(
            jax.ShapeDtypeStruct((1, rows), full),
            jax.ShapeDtypeStruct((rows, width), full),
            jax.ShapeDtypeStruct((rows, width), full),
        ),
        in_specs=[smem, smem, vmem, vmem],
        out_specs=(vmem, vmem, vmem),
        scratch_shapes=[
            pltpu.VMEM((8 * rows, width), half_type),
            pltpu.VMEM((6 * rows, width), half_type),
            pltpu.VMEM((8 * rows, 6 * rows), half_type),
            pltpu.VMEM((8 * rows, width), full),
            pltpu.VMEM((6 * rows, width), full),
            pltpu.VMEM((3, 8, 2 * rows), full),
            pltpu.VMEM((rows, width), half_type),
            pltpu.VMEM((2, rows, width), half_type),
            pltpu.VMEM((2, rows, width), half_type),
            pltpu.VMEM((2, 2, rows, width), half_type),
            pltpu.VMEM((2, 2, rows, width), half_type),
            pltpu.VMEM((rows, width), half_type),
            pltpu.VMEM((rows, width), half_type),
            pltpu.VMEM((rows, width), half_type),
            pltpu.VMEM((3, rows, width), half_type),
            pltpu.VMEM((3, rows, width), half_type),
            pltpu.VMEM((8, rows), full),
            pltpu.VMEM((8, rows), full),
            pltpu.VMEM((2, rows, width), half_type),
            pltpu.VMEM((2, rows, width), half_type),
            pltpu.VMEM((2, 8, rows), full),
            pltpu.VMEM((2, 8, rows), full),
            pltpu.SemaphoreType.DMA((N_MESSAGES,)),
            pltpu.SemaphoreType.DMA((N_MESSAGES,)),
        ],
        compiler_params=pltpu.CompilerParams(
            collective_id=0, has_side_effects=True, vmem_limit_bytes=48 * 1024 * 1024
        ),
    )(log_scale, bias, image_emb, text_emb)
    return (loss.reshape(rows), grad_image, grad_text)


def solution(mesh):
    groups = mesh.shape["outer"]
    in_specs = (P(("outer", "inner"), None), P(("outer", "inner"), None), P(), P())
    out_specs = (P(("outer", "inner")), P(("outer", "inner"), None), P(("outer", "inner"), None))
    return jax.shard_map(
        lambda *args: per_device(groups, *args),
        mesh=mesh, in_specs=in_specs, out_specs=out_specs, check_vma=False,
    )
```

time: 87.5 us -> 81.2 us (0.928)
  the two profiles are of different devices: /device:TPU:64 before, /device:TPU:72 now
where the time goes in v2:
time: 81.2 us; the launch traced here: 81 us
  Pallas kernels  75 us (92%)
  local copies, waits for them, and re-layouts  4.06 us (5%)
  between operations  1.94 us (2%)
    pallas_call x1, Pallas kernels, per_device(): pl.pallas_call(lambda *refs: kernel(groups, *refs), out_shape=(jax.ShapeD...  75 us
    unnamed x7, local copies, waits for them, and re-layouts  4.06 us

profile of v2, /device:TPU:72, one launch (start us, length us, event | category | flops | bytes accessed | tf_op | source)
XLA Modules:
  0.0 81.0 jit_solution(8084009108666250673)
XLA Ops:
  1.9 0.0 copy-start
  1.9 1.0 %copy-done = bf16[128,1152]{1,0:T(8,128)(2,1)S(1)} copy-done((bf16[128,1152]{1,0:T(8,128)(2,1)S(1)}, bf16[128,1152]{1,0:T(8,128)(2,1)}, u32[]{:S(2)}) %copy-start) | copy-done | bytes 294936
  2.9 0.0 copy-start.1
  2.9 1.0 %copy-done.1 = bf16[128,1152]{1,0:T(8,128)(2,1)S(1)} copy-done((bf16[128,1152]{1,0:T(8,128)(2,1)S(1)}, bf16[128,1152]{1,0:T(8,128)(2,1)}, u32[]{:S(2)}) %copy-start.1) | copy-done | bytes 294936
  3.8 75.0 %shard_map.67 = (f32[1,128]{1,0:T(1,128)S(1)}, f32[128,1152]{1,0:T(8,128)S(1)}, f32[128,1152]{1,0:T(8,128)S(1)}) custom-call(f32[1]{0:T(128)S(6)} %copy.10.refs_0_, f32[1]{0:T(128)S(6)} %copy.11.refs_1_, bf16[128,1152]{1,0:T(8,128)(2,1)S(1)} %copy-done, bf16[128,1152]{1,0:T(8,128)(2,1)S(1)} %copy-done.1), custom_call_target="tpu_custom_call" | custom-call | tf_op jit(solution)/shard_map/pallas_call | solution.py:336
  78.8 0.5 copy.12
  79.3 0.8 %copy.13 = f32[128,1152]{1,0:T(8,128)} copy(f32[128,1152]{1,0:T(8,128)S(1)} %get-tuple-element.13) | data formatting | bytes 1179648
  80.2 0.8 %copy.14 = f32[128,1152]{1,0:T(8,128)} copy(f32[128,1152]{1,0:T(8,128)S(1)} %get-tuple-element.14) | data formatting | bytes 1179648
Async XLA Ops:
  1.9 1.0 %copy-start = (bf16[128,1152]{1,0:T(8,128)(2,1)S(1)}, bf16[128,1152]{1,0:T(8,128)(2,1)}, u32[]{:S(2)}) copy-start(bf16[128,1152]{1,0:T(8,128)(2,1)} %refs_2_.1) | copy-start | bytes 884740
  2.9 1.0 %copy-start.1 = (bf16[128,1152]{1,0:T(8,128)(2,1)S(1)}, bf16[128,1152]{1,0:T(8,128)(2,1)}, u32[]{:S(2)}) copy-start(bf16[128,1152]{1,0:T(8,128)(2,1)} %refs_3_.1) | copy-start | bytes 884740

commit v3 on v2

--- a/solution.py
+++ b/solution.py
@@ -14,7 +14,9 @@
 
 OWN, FAR, PREV, NEXT = 0, 1, 2, 3
 
-CHUNKS = 2
+CHUNKS = 4
+UNITS = 2
+BOTH = CHUNKS // UNITS
 
 
 def unit_of(raw):
@@ -58,7 +60,8 @@
     sub = rows // CHUNKS
     half = sub // 2
     pair = 2 * rows
-    unit = 4 * sub
+    part = rows // UNITS
+    unit = 4 * part
     tile = width // 3 if width % 384 == 0 else width
     peers = places(groups)
     messages = []
@@ -73,15 +76,24 @@
         )
         return messages[-1]
 
-    def base(r, c):
-        return (r * CHUNKS + c) * unit
+    def base(r, u):
+        return (r * UNITS + u) * unit
+
+    def place(r, c, k):
+        return base(r, c // BOTH) + k * part + (c % BOTH) * sub
 
     def text(r, c, k, h):
-        return texts.at[pl.ds(base(r, c) + k * sub + h * half, half), :]
+        return texts.at[pl.ds(place(r, c, k) + h * half, half), :]
+
+    def chunk(r, c, k):
+        return texts.at[pl.ds(place(r, c, k), sub), :]
 
     def piece(c, h):
         return pl.ds(c * sub + h * half, half)
 
+    def whole_piece(c):
+        return pl.ds(c * sub, sub)
+
     def image(k):
         return images.at[pl.ds(k * rows, rows), :]
 
@@ -93,17 +105,15 @@
 
     z_out = each(lambda c, h: message(text(0, c, OWN, h), relay.at[piece(c, h), :], ("zn", "zp")[h]))
     z_on = each(lambda c, h: message(relay.at[piece(c, h), :], text(1, c, OWN, h), ("zn", "zp")[h]))
-    to_next = each_row(lambda r, c, h: message(text(r, c, OWN, h), text(r, c, PREV, h), "xn"))
-    to_prev = each_row(lambda r, c, h: message(text(r, c, OWN, h), text(r, c, NEXT, h), "xp"))
+    to_side = each_row(lambda r, c, s: message(chunk(r, c, OWN), chunk(r, c, (PREV, NEXT)[s]), ("xn", "xp")[s]))
     far_on = each_row(lambda r, c, h: message(text(r, c, (PREV, NEXT)[h], h), text(r, c, FAR, h), ("xn", "xp")[h]))
     img_next = message(image(0), image(1), "gn")
     img_prev = message(image(0), image(2), "gp")
     img_sib = [message(image(k), image(3 + k), "sib") for k in range(3)]
     far_back = each_row(lambda r, c, h: message(far_s.at[r, piece(c, h), :], far_r.at[r, piece(c, h), :], ("xp", "xn")[h]))
-    row_back = [
-        each_row(lambda r, c, h: message(row_s.at[r, s, piece(c, h), :], row_r.at[r, s, piece(c, h), :], ("xp", "xn")[s]))
-        for s in range(2)
-    ]
+    row_back = each_row(
+        lambda r, c, s: message(row_s.at[r, s, whole_piece(c), :], row_r.at[r, s, whole_piece(c), :], ("xp", "xn")[s])
+    )
     z_back = each(lambda c, h: message(col_s.at[piece(c, h), :], back.at[piece(c, h), :], ("zp", "zn")[h]))
     z_home = each(lambda c, h: message(back.at[piece(c, h), :], col_r.at[piece(c, h), :], ("zp", "zn")[h]))
     sib_back = [message(sib_s.at[k], sib_r.at[k], "sib") for k in range(3)]
@@ -117,7 +127,7 @@
 
     own = unit_of(txt_ref[...])[0].astype(jnp.bfloat16)
     for c in range(CHUNKS):
-        texts[pl.ds(base(0, c), sub), :] = own[c * sub:(c + 1) * sub]
+        texts[pl.ds(place(0, c, OWN), sub), :] = own[c * sub:(c + 1) * sub]
     images[pl.ds(0, rows), :] = unit_of(img_ref[...])[0].astype(jnp.bfloat16)
     loss_acc[...] = jnp.zeros_like(loss_acc)
     scale = jnp.exp(jnp.full((1, pair), ls_ref[0], jnp.float32))
@@ -134,7 +144,7 @@
             for copy in one:
                 copy.wait_recv()
 
-    def weigh(c, start, j, diagonal):
+    def weigh(u, start, j, diagonal):
         columns = pl.ds(j * pair, pair)
         dots = lax.dot_general(
             texts[pl.ds(start, unit), :], images[columns, :], (((1,), (1,)), ((), ())),
@@ -147,7 +157,7 @@
         if diagonal:
             row = lax.broadcasted_iota(jnp.int32, (unit, pair), 0)
             column = lax.broadcasted_iota(jnp.int32, (unit, pair), 1)
-            positive = (row + c * sub == column) & (row < sub)
+            positive = (row + u * part == column) & (row < part)
             weights = weights - positive.astype(jnp.float32)
             whole = jnp.where(positive, 1.0 + jnp.exp(-logits), whole)
         wt[pl.ds(start, unit), columns] = weights.astype(jnp.bfloat16)
@@ -155,10 +165,10 @@
         product = (whole[:q] * whole[q:2 * q]) * (whole[2 * q:3 * q] * whole[3 * q:])
         loss_acc[j] += jnp.sum(jnp.log(product).reshape(q // 8, 8, pair), axis=0)
 
-    def both(r, c):
-        begin = base(r, c)
+    def both(r, u):
+        begin = base(r, u)
         for j in range(3):
-            weigh(c, begin, j, r == 0 and j == 0)
+            weigh(u, begin, j, r == 0 and j == 0)
         for n in range(width // tile):
             columns = pl.ds(n * tile, tile)
             tg[pl.ds(begin, unit), columns] = jnp.dot(
@@ -174,7 +184,7 @@
             )
 
     def partial(r, c, k, h):
-        return tg[pl.ds(base(r, c) + k * sub + h * half, half), :]
+        return tg[pl.ds(place(r, c, k) + h * half, half), :]
 
     def reduce_begin(r, c):
         for h in range(2):
@@ -182,88 +192,85 @@
             far_back[r][c][h].start()
         for s in range(2):
             row_s[r, s, piece(c, 1 - s), :] = partial(r, c, (PREV, NEXT)[s], 1 - s).astype(jnp.bfloat16)
-            row_back[s][r][c][1 - s].start()
 
     def reduce_middle(r, c):
         for s in range(2):
             far_back[r][c][s].wait_recv()
             total = partial(r, c, (PREV, NEXT)[s], s) + far_r[r, piece(c, s), :].astype(jnp.float32)
             row_s[r, s, piece(c, s), :] = total.astype(jnp.bfloat16)
-            row_back[s][r][c][s].start()
-
-    def reduce_end(r, c, h):
-        row_back[0][r][c][h].wait_recv()
-        row_back[1][r][c][h].wait_recv()
+            row_back[r][c][s].start()
+
+    def reduce_end(r, c):
+        arrive(row_back[r][c])
         return (
-            partial(r, c, OWN, h)
-            + row_r[r, 0, piece(c, h), :].astype(jnp.float32)
-            + row_r[r, 1, piece(c, h), :].astype(jnp.float32)
+            tg[pl.ds(place(r, c, OWN), sub), :]
+            + row_r[r, 0, whole_piece(c), :].astype(jnp.float32)
+            + row_r[r, 1, whole_piece(c), :].astype(jnp.float32)
         )
 
     def column_home(c):
-        for h in range(2):
-            col_s[piece(c, h), :] = reduce_end(1, c, h).astype(jnp.bfloat16)
-            z_back[c][h].start()
+        col_s[whole_piece(c), :] = reduce_end(1, c).astype(jnp.bfloat16)
+        start(z_back[c])
+
+    def pass_on(arrivals, onward):
+        for here, there in zip(arrivals, onward):
+            here.wait_recv()
+            there.start()
 
     def loss_of(k):
         block = loss_acc[k // 2]
         return jnp.sum(block[:, (k % 2) * rows:(k % 2 + 1) * rows], axis=0, keepdims=True)
 
-    def far_forward(r, c):
-        to_next[r][c][0].wait_recv()
-        far_on[r][c][0].start()
-        to_prev[r][c][1].wait_recv()
-        far_on[r][c][1].start()
-
-    def all_here(r, c):
-        to_next[r][c][1].wait_recv()
-        to_prev[r][c][0].wait_recv()
-        arrive(far_on[r][c])
-
-    def row_out(r, c):
-        for h in range(2):
-            to_next[r][c][h].start()
-            to_prev[r][c][1 - h].start()
-
-    start(z_out[0])
+    def all_here(r, u):
+        for c in range(u * BOTH, (u + 1) * BOTH):
+            arrive(far_on[r][c])
+
+    start(z_out[0], z_out[1])
+    start(to_side[0][0])
     img_next.start()
     img_prev.start()
-    row_out(0, 0)
     img_sib[0].start()
-    row_out(0, 1)
-    for h in range(2):
-        z_out[0][h].wait_recv()
-        z_on[0][h].start()
-    far_forward(0, 0)
-    img_next.wait_recv()
-    img_sib[1].start()
-    img_prev.wait_recv()
-    img_sib[2].start()
-    start(z_out[1])
-    far_forward(0, 1)
-    arrive(z_on[0])
-    row_out(1, 0)
+    start(to_side[0][1], to_side[0][2], to_side[0][3])
+    for c in range(2):
+        pass_on(z_out[c], z_on[c])
+    pass_on(to_side[0][0], far_on[0][0])
+    pass_on(to_side[0][1], far_on[0][1])
+    for c in range(2):
+        arrive(z_on[c])
+        start(to_side[1][c])
+        start(z_out[2 + c])
+    pass_on([img_next, img_prev], img_sib[1:])
+    pass_on(to_side[0][2], far_on[0][2])
+    pass_on(to_side[0][3], far_on[0][3])
+    pass_on(z_out[2], z_on[2])
+    pass_on(to_side[1][0], far_on[1][0])
+    pass_on(z_out[3], z_on[3])
+    pass_on(to_side[1][1], far_on[1][1])
     arrive(img_sib)
     all_here(0, 0)
     both(0, 0)
-    for h in range(2):
-        z_out[1][h].wait_recv()
-        z_on[1][h].start()
-    far_forward(1, 0)
+    for c in (2, 3):
+        arrive(z_on[c])
+        start(to_side[1][c])
+    all_here(1, 0)
+    both(1, 0)
+    for c in (0, 1):
+        reduce_begin(1, c)
+    for c in (2, 3):
+        pass_on(to_side[1][c], far_on[1][c])
+    for c in (0, 1):
+        reduce_middle(1, c)
     all_here(0, 1)
     both(0, 1)
-    arrive(z_on[1])
-    row_out(1, 1)
-    all_here(1, 0)
-    both(1, 0)
-    reduce_begin(1, 0)
-    far_forward(1, 1)
-    reduce_middle(1, 0)
+    for c in (0, 1):
+        column_home(c)
     all_here(1, 1)
     both(1, 1)
 
-    reduce_begin(1, 1)
-    column_home(0)
+    for c in (2, 3):
+        reduce_begin(1, c)
+    for c in (0, 1):
+        pass_on(z_back[c], z_home[c])
     image_partial(3 * rows)
     for k in (1, 2, 0):
         sib_s[k] = ig[pl.ds((3 + k) * rows, rows), :].astype(jnp.bfloat16)
@@ -272,12 +279,11 @@
     for k in range(3):
         sib_ls[pl.ds(k, 1), :] = loss_of(3 + k)
     sib_loss.start()
-    reduce_middle(1, 1)
+    for c in (2, 3):
+        reduce_middle(1, c)
     image_partial(0)
-    for h in range(2):
-        z_back[0][h].wait_recv()
-        z_home[0][h].start()
-    column_home(1)
+    for c in (2, 3):
+        column_home(c)
     sib_loss.wait_recv()
     for s in range(2):
         sib_back[s + 1].wait_recv()
@@ -287,9 +293,8 @@
         ret_loss[s].start()
     for c in range(CHUNKS):
         reduce_begin(0, c)
-    for h in range(2):
-        z_back[1][h].wait_recv()
-        z_home[1][h].start()
+    for c in (2, 3):
+        pass_on(z_back[c], z_home[c])
     for c in range(CHUNKS):
         reduce_middle(0, c)
 
@@ -301,31 +306,32 @@
         return (grads - unit * jnp.sum(unit * grads, axis=1, keepdims=True)) * inverse
 
     def finish_text(c):
-        for h in range(2):
-            near = reduce_end(0, c, h)
-            z_home[c][h].wait_recv()
-            gt_ref[piece(c, h), :] = backprop(txt_ref[piece(c, h), :], near + col_r[piece(c, h), :].astype(jnp.float32))
+        here = whole_piece(c)
+        near = reduce_end(0, c)
+        arrive(z_home[c])
+        gt_ref[here, :] = backprop(txt_ref[here, :], near + col_r[here, :].astype(jnp.float32))
 
     finish_text(0)
+    finish_text(1)
     sib_back[0].wait_recv()
     for s in range(2):
         ret_loss[s].wait_recv()
         ret[s].wait_recv()
     loss_ref[...] = loss_of(0) + sib_lr[pl.ds(0, 1), :] + ret_lr[0, pl.ds(0, 1), :] + ret_lr[1, pl.ds(0, 1), :]
     for c in range(CHUNKS):
-        for h in range(2):
-            here = piece(c, h)
-            grads = (
-                (ig[here, :] + sib_r[0, here, :].astype(jnp.float32))
-                + (ret_r[0, here, :].astype(jnp.float32) + ret_r[1, here, :].astype(jnp.float32))
-            )
-            gi_ref[here, :] = backprop(img_ref[here, :], grads)
-    finish_text(1)
+        here = whole_piece(c)
+        grads = (
+            (ig[here, :] + sib_r[0, here, :].astype(jnp.float32))
+            + (ret_r[0, here, :].astype(jnp.float32) + ret_r[1, here, :].astype(jnp.float32))
+        )
+        gi_ref[here, :] = backprop(img_ref[here, :], grads)
+    finish_text(2)
+    finish_text(3)
     for sent in messages:
         sent.wait_send()
 
 
-N_MESSAGES = 77
+N_MESSAGES = 109
 
 
 def per_device(groups, image_emb, text_emb, log_scale, bias):

time: 81.2 us -> 84.1 us (1.036)
  the two profiles are of different devices: /device:TPU:72 before, /device:TPU:112 now
where the time goes in v3:
time: 84.1 us; the launch traced here: 83.9 us
  Pallas kernels  77.9 us (93%)
  local copies, waits for them, and re-layouts  4.06 us (5%)
  between operations  1.94 us (2%)
    pallas_call x1, Pallas kernels, per_device(): pl.pallas_call(lambda *refs: kernel(groups, *refs), out_shape=(jax.ShapeD...  77.9 us
    unnamed x7, local copies, waits for them, and re-layouts  4.06 us

profile of v3, /device:TPU:112, one launch (start us, length us, event | category | flops | bytes accessed | tf_op | source)
XLA Modules:
  0.0 83.9 jit_solution(18040036828994205338)
XLA Ops:
  1.9 0.0 copy-start
  1.9 1.0 %copy-done = bf16[128,1152]{1,0:T(8,128)(2,1)S(1)} copy-done((bf16[128,1152]{1,0:T(8,128)(2,1)S(1)}, bf16[128,1152]{1,0:T(8,128)(2,1)}, u32[]{:S(2)}) %copy-start) | copy-done | bytes 294936
  2.9 0.0 copy-start.1
  2.9 1.0 %copy-done.1 = bf16[128,1152]{1,0:T(8,128)(2,1)S(1)} copy-done((bf16[128,1152]{1,0:T(8,128)(2,1)S(1)}, bf16[128,1152]{1,0:T(8,128)(2,1)}, u32[]{:S(2)}) %copy-start.1) | copy-done | bytes 294936
  3.8 77.9 %shard_map.67 = (f32[1,128]{1,0:T(1,128)S(1)}, f32[128,1152]{1,0:T(8,128)S(1)}, f32[128,1152]{1,0:T(8,128)S(1)}) custom-call(f32[1]{0:T(128)S(6)} %copy.10.refs_0_, f32[1]{0:T(128)S(6)} %copy.11.refs_1_, bf16[128,1152]{1,0:T(8,128)(2,1)S(1)} %copy-done, bf16[128,1152]{1,0:T(8,128)(2,1)S(1)} %copy-done.1), custom_call_target="tpu_custom_call" | custom-call | tf_op jit(solution)/shard_map/pallas_call | solution.py:342
  81.8 0.5 copy.12
  82.3 0.8 copy.13
  83.1 0.8 copy.14
Async XLA Ops:
  1.9 1.0 %copy-start = (bf16[128,1152]{1,0:T(8,128)(2,1)S(1)}, bf16[128,1152]{1,0:T(8,128)(2,1)}, u32[]{:S(2)}) copy-start(bf16[128,1152]{1,0:T(8,128)(2,1)} %refs_2_.1) | copy-start | bytes 884740
  2.9 1.0 %copy-start.1 = (bf16[128,1152]{1,0:T(8,128)(2,1)S(1)}, bf16[128,1152]{1,0:T(8,128)(2,1)}, u32[]{:S(2)}) copy-start(bf16[128,1152]{1,0:T(8,128)(2,1)} %refs_3_.1) | copy-start | bytes 884740

commit v4 on v3

--- a/solution.py
+++ b/solution.py
@@ -14,7 +14,7 @@
 
 OWN, FAR, PREV, NEXT = 0, 1, 2, 3
 
-CHUNKS = 4
+CHUNKS = 2
 UNITS = 2
 BOTH = CHUNKS // UNITS
 
@@ -62,7 +62,6 @@
     pair = 2 * rows
     part = rows // UNITS
     unit = 4 * part
-    tile = width // 3 if width % 384 == 0 else width
     peers = places(groups)
     messages = []
 
@@ -169,19 +168,24 @@
         begin = base(r, u)
         for j in range(3):
             weigh(u, begin, j, r == 0 and j == 0)
-        for n in range(width // tile):
-            columns = pl.ds(n * tile, tile)
-            tg[pl.ds(begin, unit), columns] = jnp.dot(
-                wt[pl.ds(begin, unit), :], images[:, columns], preferred_element_type=jnp.float32
-            )
-
-    def image_partial(first):
-        for n in range(width // tile):
-            columns = pl.ds(n * tile, tile)
-            ig[pl.ds(first, 3 * rows), columns] = lax.dot_general(
-                wt[:, pl.ds(first, 3 * rows)], texts[:, columns], (((0,), (0,)), ((), ())),
-                preferred_element_type=jnp.float32,
-            )
+        tg[pl.ds(begin, unit), :] = jnp.dot(
+            wt[pl.ds(begin, unit), :], images[...], preferred_element_type=jnp.float32
+        )
+
+    def image_partial(r, u, first):
+        begin = base(r, u)
+        term = lax.dot_general(
+            wt[pl.ds(begin, unit), pl.ds(first, 3 * rows)], texts[pl.ds(begin, unit), :], (((0,), (0,)), ((), ())),
+            preferred_element_type=jnp.float32,
+        )
+        if r == 0 and u == 0:
+            ig[pl.ds(first, 3 * rows), :] = term
+        else:
+            ig[pl.ds(first, 3 * rows), :] += term
+
+    def image_partials(r, u):
+        image_partial(r, u, 3 * rows)
+        image_partial(r, u, 0)
 
     def partial(r, c, k, h):
         return tg[pl.ds(place(r, c, k) + h * half, half), :]
@@ -225,65 +229,51 @@
         for c in range(u * BOTH, (u + 1) * BOTH):
             arrive(far_on[r][c])
 
-    start(z_out[0], z_out[1])
-    start(to_side[0][0])
+    start(z_out[0], to_side[0][0])
     img_next.start()
     img_prev.start()
     img_sib[0].start()
-    start(to_side[0][1], to_side[0][2], to_side[0][3])
-    for c in range(2):
-        pass_on(z_out[c], z_on[c])
+    start(to_side[0][1])
+    pass_on(z_out[0], z_on[0])
     pass_on(to_side[0][0], far_on[0][0])
+    pass_on([img_next, img_prev], img_sib[1:])
     pass_on(to_side[0][1], far_on[0][1])
-    for c in range(2):
-        arrive(z_on[c])
-        start(to_side[1][c])
-        start(z_out[2 + c])
-    pass_on([img_next, img_prev], img_sib[1:])
-    pass_on(to_side[0][2], far_on[0][2])
-    pass_on(to_side[0][3], far_on[0][3])
-    pass_on(z_out[2], z_on[2])
-    pass_on(to_side[1][0], far_on[1][0])
-    pass_on(z_out[3], z_on[3])
-    pass_on(to_side[1][1], far_on[1][1])
+    arrive(z_on[0])
+    start(to_side[1][0], z_out[1])
     arrive(img_sib)
     all_here(0, 0)
     both(0, 0)
-    for c in (2, 3):
-        arrive(z_on[c])
-        start(to_side[1][c])
+    pass_on(z_out[1], z_on[1])
+    image_partials(0, 0)
+    pass_on(to_side[1][0], far_on[1][0])
+    all_here(0, 1)
+    both(0, 1)
+    arrive(z_on[1])
+    start(to_side[1][1])
+    image_partials(0, 1)
     all_here(1, 0)
     both(1, 0)
-    for c in (0, 1):
-        reduce_begin(1, c)
-    for c in (2, 3):
-        pass_on(to_side[1][c], far_on[1][c])
-    for c in (0, 1):
-        reduce_middle(1, c)
-    all_here(0, 1)
-    both(0, 1)
-    for c in (0, 1):
-        column_home(c)
+    reduce_begin(1, 0)
+    pass_on(to_side[1][1], far_on[1][1])
+    image_partials(1, 0)
+    reduce_middle(1, 0)
     all_here(1, 1)
     both(1, 1)
 
-    for c in (2, 3):
-        reduce_begin(1, c)
-    for c in (0, 1):
-        pass_on(z_back[c], z_home[c])
-    image_partial(3 * rows)
+    reduce_begin(1, 1)
+    column_home(0)
+    image_partial(1, 1, 3 * rows)
     for k in (1, 2, 0):
         sib_s[k] = ig[pl.ds((3 + k) * rows, rows), :].astype(jnp.bfloat16)
         sib_back[k].start()
+    reduce_middle(1, 1)
     sib_ls[...] = jnp.zeros_like(sib_ls)
     for k in range(3):
         sib_ls[pl.ds(k, 1), :] = loss_of(3 + k)
     sib_loss.start()
-    for c in (2, 3):
-        reduce_middle(1, c)
-    image_partial(0)
-    for c in (2, 3):
-        column_home(c)
+    image_partial(1, 1, 0)
+    pass_on(z_back[0], z_home[0])
+    column_home(1)
     sib_loss.wait_recv()
     for s in range(2):
         sib_back[s + 1].wait_recv()
@@ -293,8 +283,7 @@
         ret_loss[s].start()
     for c in range(CHUNKS):
         reduce_begin(0, c)
-    for c in (2, 3):
-        pass_on(z_back[c], z_home[c])
+    pass_on(z_back[1], z_home[1])
     for c in range(CHUNKS):
         reduce_middle(0, c)
 
@@ -312,7 +301,6 @@
         gt_ref[here, :] = backprop(txt_ref[here, :], near + col_r[here, :].astype(jnp.float32))
 
     finish_text(0)
-    finish_text(1)
     sib_back[0].wait_recv()
     for s in range(2):
         ret_loss[s].wait_recv()
@@ -325,13 +313,12 @@
             + (ret_r[0, here, :].astype(jnp.float32) + ret_r[1, here, :].astype(jnp.float32))
         )
         gi_ref[here, :] = backprop(img_ref[here, :], grads)
-    finish_text(2)
-    finish_text(3)
+    finish_text(1)
     for sent in messages:
         sent.wait_send()
 
 
-N_MESSAGES = 109
+N_MESSAGES = 61
 
 
 def per_device(groups, image_emb, text_emb, log_scale, bias):

time: 84.1 us -> 86 us (1.023)
  the two profiles are of different devices: /device:TPU:112 before, /device:TPU:4 now
where the time goes in v4:
time: 86 us; the launch traced here: 85.8 us
  Pallas kernels  79.8 us (93%)
  local copies, waits for them, and re-layouts  4.06 us (5%)
  between operations  1.94 us (2%)
    pallas_call x1, Pallas kernels, per_device(): pl.pallas_call(lambda *refs: kernel(groups, *refs), out_shape=(jax.ShapeD...  79.8 us
    unnamed x7, local copies, waits for them, and re-layouts  4.06 us

profile of v4, /device:TPU:4, one launch (start us, length us, event | category | flops | bytes accessed | tf_op | source)
XLA Modules:
  0.0 85.8 jit_solution(17436140224741282313)
XLA Ops:
  1.9 0.0 copy-start
  1.9 1.0 %copy-done = bf16[128,1152]{1,0:T(8,128)(2,1)S(1)} copy-done((bf16[128,1152]{1,0:T(8,128)(2,1)S(1)}, bf16[128,1152]{1,0:T(8,128)(2,1)}, u32[]{:S(2)}) %copy-start) | copy-done | bytes 294936
  2.9 0.0 copy-start.1
  2.9 1.0 %copy-done.1 = bf16[128,1152]{1,0:T(8,128)(2,1)S(1)} copy-done((bf16[128,1152]{1,0:T(8,128)(2,1)S(1)}, bf16[128,1152]{1,0:T(8,128)(2,1)}, u32[]{:S(2)}) %copy-start.1) | copy-done | bytes 294936
  3.8 79.8 %shard_map.67 = (f32[1,128]{1,0:T(1,128)S(1)}, f32[128,1152]{1,0:T(8,128)S(1)}, f32[128,1152]{1,0:T(8,128)S(1)}) custom-call(f32[1]{0:T(128)S(6)} %copy.10.refs_0_, f32[1]{0:T(128)S(6)} %copy.11.refs_1_, bf16[128,1152]{1,0:T(8,128)(2,1)S(1)} %copy-done, bf16[128,1152]{1,0:T(8,128)(2,1)S(1)} %copy-done.1), custom_call_target="tpu_custom_call" | custom-call | tf_op jit(solution)/shard_map/pallas_call | solution.py:329
  83.7 0.5 copy.12
  84.2 0.8 copy.13
  85.0 0.8 copy.14
Async XLA Ops:
  1.9 1.0 %copy-start = (bf16[128,1152]{1,0:T(8,128)(2,1)S(1)}, bf16[128,1152]{1,0:T(8,128)(2,1)}, u32[]{:S(2)}) copy-start(bf16[128,1152]{1,0:T(8,128)(2,1)} %refs_2_.1) | copy-start | bytes 884740
  2.9 1.0 %copy-start.1 = (bf16[128,1152]{1,0:T(8,128)(2,1)S(1)}, bf16[128,1152]{1,0:T(8,128)(2,1)}, u32[]{:S(2)}) copy-start(bf16[128,1152]{1,0:T(8,128)(2,1)} %refs_3_.1) | copy-start | bytes 884740

commit v5 on v0

v5 whole, which is shorter than its diff:
```python
import jax
import jax.numpy as jnp
from jax import lax
from jax.experimental import pallas as pl
from jax.experimental.pallas import tpu as pltpu
from jax.sharding import PartitionSpec as P

MESH = pl.DeviceIdType.MESH
EPS = 1e-06

X_N = 4
Z_LO = 4
Z_N = 8

OWN, FAR, PREV, NEXT = 0, 1, 2, 3
UP1, DOWN1, UP3, DOWN3, OVER = 1, 2, 3, 4, 5

CHUNKS = 2
PARTS = 2


def unit_of(raw):
    wide = raw.astype(jnp.float32)
    inverse = lax.rsqrt(jnp.sum(wide * wide, axis=1, keepdims=True) + EPS)
    return wide * inverse, inverse


def places(groups):
    outer = lax.axis_index("outer")
    inner = lax.axis_index("inner")
    z_lo = outer % Z_LO
    x, z_hi, core = inner // 4, (inner // 2) % 2, inner % 2

    def inner_of(x, z_hi, core):
        return x * 4 + z_hi * 2 + core

    def group_by(by):
        z = (z_hi * Z_LO + z_lo + by + Z_N) % Z_N
        step = by if by in (1, -1) else -by
        return ((outer + step + groups) % groups, inner_of(x, z // Z_LO, core))

    return {
        "xn": (outer, inner_of((x + 1) % X_N, z_hi, core)),
        "xp": (outer, inner_of((x + X_N - 1) % X_N, z_hi, core)),
        "sib": (outer, inner_of(x, z_hi, 1 - core)),
        "gn": group_by(1),
        "gp": group_by(-1),
        "tn": group_by(2),
        "tp": group_by(-2),
    }


def kernel(
    groups, ls_ref, b_ref, img_ref, txt_ref, loss_ref, gi_ref, gt_ref,
    texts, images, wt, tg, ig, loss_acc, over_s, over_r, three_s, three_r, one_s, one_r,
    sib_s, sib_r, far_s, far_r, row_s, row_r, over_ls, over_lr, three_ls, three_lr, one_ls, one_lr, ssem, rsem,
):
    rows, width = img_ref.shape
    sub = rows // CHUNKS
    half = sub // 2
    part = rows // PARTS
    edge = part // 2
    tile = 2 * rows
    row_texts = 4 * rows
    peers = places(groups)
    messages = []

    def message(src, dst, peer):
        index = len(messages)
        messages.append(
            pltpu.make_async_remote_copy(
                src_ref=src, dst_ref=dst, send_sem=ssem.at[index], recv_sem=rsem.at[index],
                device_id=peers[peer], device_id_type=MESH,
            )
        )
        return messages[-1]

    def at(c, k, h=0):
        return (c * 6 + k) * sub + h * half

    def image(c, k):
        return images.at[pl.ds(at(c, k), sub), :]

    def image_half(c, k, h):
        return images.at[pl.ds(at(c, k, h), half), :]

    def text(q, j):
        return texts.at[pl.ds((q * 4 + j) * rows, rows), :]

    def text_part(j, p):
        return texts.at[pl.ds(j * rows + p * part, part), :]

    def text_edge(j, p, e):
        return texts.at[pl.ds(j * rows + p * part + e * edge, edge), :]

    def halves(h):
        return pl.ds(h * half, half)

    def parts(p):
        return pl.ds(p * part, part)

    def edges(p, e):
        return pl.ds(p * part + e * edge, edge)

    z1 = [[message(image(c, OWN), image(c, UP1), "gn"), message(image(c, OWN), image(c, DOWN1), "gp")] for c in range(CHUNKS)]
    z3 = [[message(image(c, UP1), image(c, UP3), "tn"), message(image(c, DOWN1), image(c, DOWN3), "tp")] for c in range(CHUNKS)]
    z4 = [
        [message(image_half(c, UP3, 0), image_half(c, OVER, 0), "gn"), message(image_half(c, DOWN3, 1), image_half(c, OVER, 1), "gp")]
        for c in range(CHUNKS)
    ]
    x1 = [[message(text_part(OWN, p), text_part((PREV, NEXT)[s], p), ("xn", "xp")[s]) for s in range(2)] for p in range(PARTS)]
    x2 = [
        [message(text_edge((PREV, NEXT)[s], p, s), text_edge(FAR, p, s), ("xn", "xp")[s]) for s in range(2)]
        for p in range(PARTS)
    ]
    across = [message(text(0, j), text(1, j), "sib") for j in range(4)]
    b4 = [[message(over_s.at[c, halves(h), :], over_r.at[c, halves(h), :], ("gp", "gn")[h]) for h in range(2)] for c in range(CHUNKS)]
    b3 = [[message(three_s.at[c, h], three_r.at[c, h], ("tp", "tn")[h]) for h in range(2)] for c in range(CHUNKS)]
    b1 = [[message(one_s.at[c, h], one_r.at[c, h], ("gp", "gn")[h]) for h in range(2)] for c in range(CHUNKS)]
    back = [[message(sib_s.at[j, parts(p), :], sib_r.at[j, parts(p), :], "sib") for j in range(4)] for p in range(PARTS)]
    t2 = [[message(far_s.at[edges(p, s), :], far_r.at[edges(p, s), :], ("xp", "xn")[s]) for s in range(2)] for p in range(PARTS)]
    t1 = [[message(row_s.at[s, parts(p), :], row_r.at[s, parts(p), :], ("xp", "xn")[s]) for s in range(2)] for p in range(PARTS)]
    l4 = [message(over_ls, over_lr.at[h], ("gp", "gn")[h]) for h in range(2)]
    l3 = [message(three_ls.at[h], three_lr.at[h], ("tp", "tn")[h]) for h in range(2)]
    l1 = [message(one_ls.at[h], one_lr.at[h], ("gp", "gn")[h]) for h in range(2)]

    def start(copies):
        for copy in copies:
            copy.start()

    def arrive(copies):
        for copy in copies:
            copy.wait_recv()

    def pass_on(arrivals, onward):
        for here, there in zip(arrivals, onward):
            here.wait_recv()
            there.start()

    barrier = pltpu.get_barrier_semaphore()
    for peer in peers.values():
        pl.semaphore_signal(barrier, inc=1, device_id=peer, device_id_type=MESH)
    own = unit_of(img_ref[...])[0].astype(jnp.bfloat16)
    for c in range(CHUNKS):
        images[pl.ds(at(c, OWN), sub), :] = own[c * sub:(c + 1) * sub]
    texts[pl.ds(0, rows), :] = unit_of(txt_ref[...])[0].astype(jnp.bfloat16)
    scale = jnp.exp(jnp.full((1, tile), ls_ref[0], jnp.float32))
    offset = b_ref[0]
    pl.semaphore_wait(barrier, len(peers))

    def weigh(begin, size, c, diagonal):
        here = pl.ds(begin, size)
        product = None
        for n in range(4):
            columns = pl.ds(n * tile, tile)
            dots = lax.dot_general(
                images[here, :], texts[columns, :], (((1,), (1,)), ((), ())), preferred_element_type=jnp.float32
            )
            logits = scale * dots + offset
            grown = jnp.exp(logits)
            whole = 1.0 + grown
            weights = grown / whole
            if diagonal and n == 0:
                row = lax.broadcasted_iota(jnp.int32, (size, tile), 0)
                column = lax.broadcasted_iota(jnp.int32, (size, tile), 1)
                positive = (row + c * sub == column) & (row < sub)
                weights = weights - positive.astype(jnp.float32)
                whole = jnp.where(positive, 1.0 + jnp.exp(-logits), whole)
            wt[here, columns] = weights.astype(jnp.bfloat16)
            product = whole if product is None else product * whole
        logs = jnp.log(product)
        loss_acc[here, :] = logs[:, :rows] + logs[:, rows:]
        ig[here, :] = jnp.dot(wt[here, :], texts[...], preferred_element_type=jnp.float32)

    def text_partial(c, q):
        these = pl.ds(at(c, 0), 6 * sub)
        columns = pl.ds(q * row_texts, row_texts)
        term = lax.dot_general(
            wt[these, columns], images[these, :], (((0,), (0,)), ((), ())), preferred_element_type=jnp.float32
        )
        if c == 0:
            tg[columns, :] = term
        else:
            tg[columns, :] += term

    def gradient(c, k):
        return ig[pl.ds(at(c, k), sub), :]

    def begin_back(c):
        over_s[c] = gradient(c, OVER).astype(jnp.bfloat16)
        start(b4[c])

    def middle_back(c):
        for h in range(2):
            b4[c][h].wait_recv()
            k = (UP3, DOWN3)[h]
            came = pl.ds(at(c, k, h), half)
            kept = pl.ds(at(c, k, 1 - h), half)
            three_s[c, h, halves(h), :] = (ig[came, :] + over_r[c, halves(h), :].astype(jnp.float32)).astype(jnp.bfloat16)
            three_s[c, h, halves(1 - h), :] = ig[kept, :].astype(jnp.bfloat16)
            b3[c][h].start()

    def end_back(c):
        for h in range(2):
            b3[c][h].wait_recv()
            one_s[c, h] = (gradient(c, (UP1, DOWN1)[h]) + three_r[c, h].astype(jnp.float32)).astype(jnp.bfloat16)
            b1[c][h].start()

    def loss_of(k):
        block = jnp.concatenate([loss_acc[pl.ds(at(c, k), sub), :] for c in range(CHUNKS)], axis=0)
        return jnp.sum(block.T, axis=0, keepdims=True)

    def give_loss(dst, row):
        dst[...] = jnp.broadcast_to(row, dst.shape)

    def partial(j, where):
        return tg[pl.ds(j * rows + where.start, where.size), :] + sib_r[j, where, :].astype(jnp.float32)

    def text_begin(p):
        arrive([back[p][FAR]])
        for s in range(2):
            far_s[edges(p, s), :] = partial(FAR, edges(p, s)).astype(jnp.bfloat16)
            t2[p][s].start()

    def text_middle(p):
        for s in range(2):
            j = (PREV, NEXT)[s]
            arrive([back[p][j]])
            row_s[s, edges(p, 1 - s), :] = partial(j, edges(p, 1 - s)).astype(jnp.bfloat16)
            t2[p][s].wait_recv()
            total = partial(j, edges(p, s)) + far_r[edges(p, s), :].astype(jnp.float32)
            row_s[s, edges(p, s), :] = total.astype(jnp.bfloat16)
            t1[p][s].start()

    for c in range(CHUNKS):
        start(z1[c])
    for p in range(PARTS):
        start(x1[p])
    across[OWN].start()
    pass_on(z1[0], z3[0])
    for p in range(PARTS):
        pass_on(x1[p], x2[p])
    across[PREV].start()
    across[NEXT].start()
    pass_on(z1[1], z3[1])
    for p in range(PARTS):
        arrive(x2[p])
    across[FAR].start()
    arrive(across)
    weigh(at(0, OWN), 3 * sub, 0, True)
    pass_on(z3[0], z4[0])
    weigh(at(0, UP3), 2 * sub, 0, False)
    weigh(at(1, OWN), 3 * sub, 1, True)
    arrive(z4[0])
    weigh(at(0, OVER), sub, 0, False)
    begin_back(0)
    pass_on(z3[1], z4[1])
    weigh(at(1, UP3), 2 * sub, 1, False)
    middle_back(0)
    for q in (1, 0):
        text_partial(0, q)
    arrive(z4[1])
    weigh(at(1, OVER), sub, 1, False)
    begin_back(1)

    end_back(0)
    text_partial(1, 1)
    for p in range(PARTS):
        for j in (FAR, PREV, NEXT, OWN):
            sib_s[j, parts(p), :] = tg[pl.ds(row_texts + j * rows + p * part, part), :].astype(jnp.bfloat16)
            back[p][j].start()
    give_loss(over_ls, loss_of(OVER))
    start(l4)
    middle_back(1)
    text_partial(1, 0)
    for p in range(PARTS):
        text_begin(p)
    lane = lax.broadcasted_iota(jnp.int32, (1, rows), 1)
    for h in range(2):
        l4[h].wait_recv()
        mine = (lane // half) % 2 == h
        give_loss(three_ls.at[h], loss_of((UP3, DOWN3)[h]) + jnp.where(mine, over_lr[h, pl.ds(0, 1), :], 0.0))
        l3[h].start()
    end_back(1)
    for p in range(PARTS):
        text_middle(p)
    for h in range(2):
        l3[h].wait_recv()
        give_loss(one_ls.at[h], loss_of((UP1, DOWN1)[h]) + three_lr[h, pl.ds(0, 1), :])
        l1[h].start()

    scale_row = jnp.exp(jnp.full((1, width), ls_ref[0], jnp.float32))

    def backprop(raw, grads):
        unit, inverse = unit_of(raw)
        grads = scale_row * grads
        return (grads - unit * jnp.sum(unit * grads, axis=1, keepdims=True)) * inverse

    def finish_image(c):
        here = pl.ds(c * sub, sub)
        arrive(b1[c])
        grads = gradient(c, OWN) + (one_r[c, 0].astype(jnp.float32) + one_r[c, 1].astype(jnp.float32))
        gi_ref[here, :] = backprop(img_ref[here, :], grads)

    def finish_text(p):
        here = parts(p)
        arrive([back[p][OWN]])
        arrive(t1[p])
        grads = partial(OWN, here) + (row_r[0, here, :].astype(jnp.float32) + row_r[1, here, :].astype(jnp.float32))
        gt_ref[here, :] = backprop(txt_ref[here, :], grads)

    finish_image(0)
    for p in range(PARTS):
        finish_text(p)
    arrive(l1)
    loss_ref[...] = loss_of(OWN) + one_lr[0, pl.ds(0, 1), :] + one_lr[1, pl.ds(0, 1), :]
    finish_image(1)
    for sent in messages:
        sent.wait_send()


N_MESSAGES = 58


def per_device(groups, image_emb, text_emb, log_scale, bias):
    rows, width = image_emb.shape
    sub = rows // CHUNKS
    half_type, full = jnp.bfloat16, jnp.float32
    vmem = pl.BlockSpec(memory_space=pltpu.VMEM)
    smem = pl.BlockSpec(memory_space=pltpu.SMEM)
    loss, grad_image, grad_text = pl.pallas_call(
        lambda *refs: kernel(groups, *refs),
        out_shape=(
            jax.ShapeDtypeStruct((1, rows), full),
            jax.ShapeDtypeStruct((rows, width), full),
            jax.ShapeDtypeStruct((rows, width), full),
        ),
        in_specs=[smem, smem, vmem, vmem],
        out_specs=(vmem, vmem, vmem),
        scratch_shapes=[
            pltpu.VMEM((8 * rows, width), half_type),
            pltpu.VMEM((6 * rows, width), half_type),
            pltpu.VMEM((6 * rows, 8 * rows), half_type),
            pltpu.VMEM((8 * rows, width), full),
            pltpu.VMEM((6 * rows, width), full),
            pltpu.VMEM((6 * rows, rows), full),
            pltpu.VMEM((CHUNKS, sub, width), half_type),
            pltpu.VMEM((CHUNKS, sub, width), half_type),
            pltpu.VMEM((CHUNKS, 2, sub, width), half_type),
            pltpu.VMEM((CHUNKS, 2, sub, width), half_type),
            pltpu.VMEM((CHUNKS, 2, sub, width), half_type),
            pltpu.VMEM((CHUNKS, 2, sub, width), half_type),
            pltpu.VMEM((4, rows, width), half_type),
            pltpu.VMEM((4, rows, width), half_type),
            pltpu.VMEM((rows, width), half_type),
            pltpu.VMEM((rows, width), half_type),
            pltpu.VMEM((2, rows, width), half_type),
            pltpu.VMEM((2, rows, width), half_type),
            pltpu.VMEM((8, rows), full),
            pltpu.VMEM((2, 8, rows), full),
            pltpu.VMEM((2, 8, rows), full),
            pltpu.VMEM((2, 8, rows), full),
            pltpu.VMEM((2, 8, rows), full),
            pltpu.VMEM((2, 8, rows), full),
            pltpu.SemaphoreType.DMA((N_MESSAGES,)),
            pltpu.SemaphoreType.DMA((N_MESSAGES,)),
        ],
        compiler_params=pltpu.CompilerParams(
            collective_id=0, has_side_effects=True, vmem_limit_bytes=48 * 1024 * 1024
        ),
    )(log_scale, bias, image_emb, text_emb)
    return (loss.reshape(rows), grad_image, grad_text)


def solution(mesh):
    groups = mesh.shape["outer"]
    in_specs = (P(("outer", "inner"), None), P(("outer", "inner"), None), P(), P())
    out_specs = (P(("outer", "inner")), P(("outer", "inner"), None), P(("outer", "inner"), None))
    return jax.shard_map(
        lambda *args: per_device(groups, *args),
        mesh=mesh, in_specs=in_specs, out_specs=out_specs, check_vma=False,
    )
```

time: 299 us -> 86.2 us (0.29)
  waiting for transfers between devices: 190 us -> 0 us
  Pallas kernels: 0 us -> 79.9 us
  starting transfers between devices: 45.8 us -> 0 us
  matrix products: 37.1 us -> 0 us
  between operations: 15.7 us -> 1.94 us
  other arithmetic: 8.94 us -> 0 us
  local copies, waits for them, and re-layouts: 0.54 us -> 4.06 us
    all_gather x2 -> x0, waiting for transfers between devices: 141 us -> none  [the longest x1 85.3 us: per_device(): texts = lax.all_gather(zt, 'inner', axis=0, tiled=True)]
    pallas_call x0 -> x1, Pallas kernels: none -> 79.9 us  [per_device(): pl.pallas_call(lambda *refs: kernel(groups, *refs), out_shape=(jax.ShapeD...]
    ppermute x15 -> x0, waiting for transfers between devices: 48.8 us -> none  [passed_along(): lax.ppermute(value, axis, [(i, (i + by) % length) for i in range(length)])]
    ppermute x15 -> x0, starting transfers between devices: 45.8 us -> none  [passed_along(): lax.ppermute(value, axis, [(i, (i + by) % length) for i in range(length)])]
    dot_general x9 -> x0, matrix products: 37.1 us -> none  [the longest x6 23.7 us: tile_terms(): jnp.dot(weights, partners, preferred_element_type=jnp.float32)]
    convert_element_type x2 -> x0, other arithmetic: 3.6 us -> none  [normalize(): return (unit, inverse, unit.astype(jnp.bfloat16))]
    unnamed x13 -> x7, local copies, waits for them, and re-layouts: 0.54 us -> 4.06 us
  transfers between devices with their start and end apart: 17 -> 0, of which waited for: 10 -> 0; matrix products, arithmetic and copies ran while one was open for 14% -> 0% of each run, Pallas kernels for 0% -> 0%
where the time goes in v5:
time: 86.2 us; the launch traced here: 85.9 us
  Pallas kernels  79.9 us (93%)
  local copies, waits for them, and re-layouts  4.06 us (5%)
  between operations  1.94 us (2%)
    pallas_call x1, Pallas kernels, per_device(): pl.pallas_call(lambda *refs: kernel(groups, *refs), out_shape=(jax.ShapeD...  79.9 us
    unnamed x7, local copies, waits for them, and re-layouts  4.06 us

profile of v5, /device:TPU:6, one launch (start us, length us, event | category | flops | bytes accessed | tf_op | source)
XLA Modules:
  0.0 85.9 jit_solution(13811374035753546385)
XLA Ops:
  1.9 0.0 copy-start
  1.9 1.0 %copy-done = bf16[128,1152]{1,0:T(8,128)(2,1)S(1)} copy-done((bf16[128,1152]{1,0:T(8,128)(2,1)S(1)}, bf16[128,1152]{1,0:T(8,128)(2,1)}, u32[]{:S(2)}) %copy-start) | copy-done | bytes 294936
  2.9 0.0 copy-start.1
  2.9 1.0 %copy-done.1 = bf16[128,1152]{1,0:T(8,128)(2,1)S(1)} copy-done((bf16[128,1152]{1,0:T(8,128)(2,1)S(1)}, bf16[128,1152]{1,0:T(8,128)(2,1)}, u32[]{:S(2)}) %copy-start.1) | copy-done | bytes 294936
  3.8 79.9 %shard_map.67 = (f32[1,128]{1,0:T(1,128)S(1)}, f32[128,1152]{1,0:T(8,128)S(1)}, f32[128,1152]{1,0:T(8,128)S(1)}) custom-call(f32[1]{0:T(128)S(6)} %copy.10.refs_0_, f32[1]{0:T(128)S(6)} %copy.11.refs_1_, bf16[128,1152]{1,0:T(8,128)(2,1)S(1)} %copy-done, bf16[128,1152]{1,0:T(8,128)(2,1)S(1)} %copy-done.1), custom_call_target="tpu_custom_call" | custom-call | tf_op jit(solution)/shard_map/pallas_call | solution.py:331
  83.8 0.5 copy.12
  84.3 0.8 copy.13
  85.1 0.8 copy.14
Async XLA Ops:
  1.9 1.0 %copy-start = (bf16[128,1152]{1,0:T(8,128)(2,1)S(1)}, bf16[128,1152]{1,0:T(8,128)(2,1)}, u32[]{:S(2)}) copy-start(bf16[128,1152]{1,0:T(8,128)(2,1)} %refs_2_.1) | copy-start | bytes 884740
  2.9 1.0 %copy-start.1 = (bf16[128,1152]{1,0:T(8,128)(2,1)S(1)}, bf16[128,1152]{1,0:T(8,128)(2,1)}, u32[]{:S(2)}) copy-start(bf16[128,1152]{1,0:T(8,128)(2,1)} %refs_3_.1) | copy-start | bytes 884740

commit v6 on v5

--- a/solution.py
+++ b/solution.py
@@ -7,6 +7,7 @@
 
 MESH = pl.DeviceIdType.MESH
 EPS = 1e-06
+LOG2_E = 1.4426950408889634
 
 X_N = 4
 Z_LO = 4
@@ -16,7 +17,7 @@
 UP1, DOWN1, UP3, DOWN3, OVER = 1, 2, 3, 4, 5
 
 CHUNKS = 2
-PARTS = 2
+PARTS = 1
 
 
 def unit_of(raw):
@@ -76,7 +77,7 @@
         return messages[-1]
 
     def at(c, k, h=0):
-        return (c * 6 + k) * sub + h * half
+        return (c * 3 + k % 3) * sub + (k // 3) * 3 * rows + h * half
 
     def image(c, k):
         return images.at[pl.ds(at(c, k), sub), :]
@@ -144,44 +145,56 @@
     for c in range(CHUNKS):
         images[pl.ds(at(c, OWN), sub), :] = own[c * sub:(c + 1) * sub]
     texts[pl.ds(0, rows), :] = unit_of(txt_ref[...])[0].astype(jnp.bfloat16)
-    scale = jnp.exp(jnp.full((1, tile), ls_ref[0], jnp.float32))
-    offset = b_ref[0]
+    scale = jnp.exp(jnp.full((1, tile), ls_ref[0], jnp.float32)) * LOG2_E
+    offset = b_ref[0] * LOG2_E
     pl.semaphore_wait(barrier, len(peers))
 
-    def weigh(begin, size, c, diagonal):
+    def weigh(begin, size, n, diagonal):
         here = pl.ds(begin, size)
-        product = None
-        for n in range(4):
-            columns = pl.ds(n * tile, tile)
-            dots = lax.dot_general(
-                images[here, :], texts[columns, :], (((1,), (1,)), ((), ())), preferred_element_type=jnp.float32
-            )
-            logits = scale * dots + offset
-            grown = jnp.exp(logits)
-            whole = 1.0 + grown
-            weights = grown / whole
-            if diagonal and n == 0:
-                row = lax.broadcasted_iota(jnp.int32, (size, tile), 0)
-                column = lax.broadcasted_iota(jnp.int32, (size, tile), 1)
-                positive = (row + c * sub == column) & (row < sub)
-                weights = weights - positive.astype(jnp.float32)
-                whole = jnp.where(positive, 1.0 + jnp.exp(-logits), whole)
-            wt[here, columns] = weights.astype(jnp.bfloat16)
-            product = whole if product is None else product * whole
-        logs = jnp.log(product)
+        columns = pl.ds(n * tile, tile)
+        dots = lax.dot_general(
+            images[here, :], texts[columns, :], (((1,), (1,)), ((), ())), preferred_element_type=jnp.float32
+        )
+        grown = jnp.exp2(scale * dots + offset)
+        whole = 1.0 + grown
+        inverse = pl.reciprocal(whole, approx=True)
+        weights = grown * (inverse * (2.0 - whole * inverse))
+        if diagonal:
+            row = lax.broadcasted_iota(jnp.int32, (size, tile), 0)
+            column = lax.broadcasted_iota(jnp.int32, (size, tile), 1)
+            positive = row < 0
+            for c in range(CHUNKS):
+                first = at(c, OWN)
+                positive |= (row - first == column - c * sub) & (row >= first) & (row < first + sub)
+            weights = weights - positive.astype(jnp.float32)
+            whole = jnp.where(positive, 1.0 + 1.0 / grown, whole)
+        wt[here, columns] = weights.astype(jnp.bfloat16)
+        return whole
+
+    def loss_part(begin, size, wholes):
+        here = pl.ds(begin, size)
+        logs = jnp.log((wholes[0] * wholes[1]) * (wholes[2] * wholes[3]))
         loss_acc[here, :] = logs[:, :rows] + logs[:, rows:]
+
+    def image_partial(begin, size):
+        here = pl.ds(begin, size)
         ig[here, :] = jnp.dot(wt[here, :], texts[...], preferred_element_type=jnp.float32)
 
-    def text_partial(c, q):
-        these = pl.ds(at(c, 0), 6 * sub)
+    def far(c):
+        begin, size = at(c, UP3), 3 * sub
+        loss_part(begin, size, [weigh(begin, size, n, False) for n in range(4)])
+        image_partial(begin, size)
+
+    def text_partial(far_ones, q):
+        these = pl.ds(far_ones * 3 * rows, 3 * rows)
         columns = pl.ds(q * row_texts, row_texts)
         term = lax.dot_general(
             wt[these, columns], images[these, :], (((0,), (0,)), ((), ())), preferred_element_type=jnp.float32
         )
-        if c == 0:
+        if far_ones:
+            tg[columns, :] += term
+        else:
             tg[columns, :] = term
-        else:
-            tg[columns, :] += term
 
     def gradient(c, k):
         return ig[pl.ds(at(c, k), sub), :]
@@ -243,47 +256,48 @@
     across[PREV].start()
     across[NEXT].start()
     pass_on(z1[1], z3[1])
+    wholes = [weigh(0, 3 * rows, 1, False)]
+    arrive([across[PREV], across[NEXT]])
+    wholes.append(weigh(0, 3 * rows, 3, False))
     for p in range(PARTS):
         arrive(x2[p])
     across[FAR].start()
-    arrive(across)
-    weigh(at(0, OWN), 3 * sub, 0, True)
+    wholes.append(weigh(0, 3 * rows, 0, True))
+    arrive([across[OWN], across[FAR]])
+    wholes.append(weigh(0, 3 * rows, 2, False))
+    loss_part(0, 3 * rows, wholes)
     pass_on(z3[0], z4[0])
-    weigh(at(0, UP3), 2 * sub, 0, False)
-    weigh(at(1, OWN), 3 * sub, 1, True)
-    arrive(z4[0])
-    weigh(at(0, OVER), sub, 0, False)
-    begin_back(0)
+    image_partial(0, 3 * rows)
     pass_on(z3[1], z4[1])
-    weigh(at(1, UP3), 2 * sub, 1, False)
-    middle_back(0)
     for q in (1, 0):
         text_partial(0, q)
-    arrive(z4[1])
-    weigh(at(1, OVER), sub, 1, False)
-    begin_back(1)
-
-    end_back(0)
+    for c in range(CHUNKS):
+        arrive(z4[c])
+        far(c)
+        begin_back(c)
+
+    middle_back(0)
     text_partial(1, 1)
     for p in range(PARTS):
         for j in (FAR, PREV, NEXT, OWN):
             sib_s[j, parts(p), :] = tg[pl.ds(row_texts + j * rows + p * part, part), :].astype(jnp.bfloat16)
             back[p][j].start()
+    middle_back(1)
     give_loss(over_ls, loss_of(OVER))
     start(l4)
-    middle_back(1)
     text_partial(1, 0)
     for p in range(PARTS):
         text_begin(p)
+    end_back(0)
     lane = lax.broadcasted_iota(jnp.int32, (1, rows), 1)
     for h in range(2):
         l4[h].wait_recv()
         mine = (lane // half) % 2 == h
         give_loss(three_ls.at[h], loss_of((UP3, DOWN3)[h]) + jnp.where(mine, over_lr[h, pl.ds(0, 1), :], 0.0))
         l3[h].start()
+    for p in range(PARTS):
+        text_middle(p)
     end_back(1)
-    for p in range(PARTS):
-        text_middle(p)
     for h in range(2):
         l3[h].wait_recv()
         give_loss(one_ls.at[h], loss_of((UP1, DOWN1)[h]) + three_lr[h, pl.ds(0, 1), :])
@@ -309,9 +323,9 @@
         grads = partial(OWN, here) + (row_r[0, here, :].astype(jnp.float32) + row_r[1, here, :].astype(jnp.float32))
         gt_ref[here, :] = backprop(txt_ref[here, :], grads)
 
+    for p in range(PARTS):
+        finish_text(p)
     finish_image(0)
-    for p in range(PARTS):
-        finish_text(p)
     arrive(l1)
     loss_ref[...] = loss_of(OWN) + one_lr[0, pl.ds(0, 1), :] + one_lr[1, pl.ds(0, 1), :]
     finish_image(1)
@@ -319,7 +333,7 @@
         sent.wait_send()
 
 
-N_MESSAGES = 58
+N_MESSAGES = 46
 
 
 def per_device(groups, image_emb, text_emb, log_scale, bias):

time: 86.2 us -> 84.9 us (0.985)
  the two profiles are of different devices: /device:TPU:6 before, /device:TPU:2 now
where the time goes in v6:
time: 84.9 us; the launch traced here: 84.7 us
  Pallas kernels  78.7 us (93%)
  local copies, waits for them, and re-layouts  4.06 us (5%)
  between operations  1.94 us (2%)
    pallas_call x1, Pallas kernels, per_device(): pl.pallas_call(lambda *refs: kernel(groups, *refs), out_shape=(jax.ShapeD...  78.7 us
    unnamed x7, local copies, waits for them, and re-layouts  4.06 us

profile of v6, /device:TPU:2, one launch (start us, length us, event | category | flops | bytes accessed | tf_op | source)
XLA Modules:
  0.0 84.7 jit_solution(387182656844250618)
XLA Ops:
  1.9 0.0 copy-start
  1.9 1.0 %copy-done = bf16[128,1152]{1,0:T(8,128)(2,1)S(1)} copy-done((bf16[128,1152]{1,0:T(8,128)(2,1)S(1)}, bf16[128,1152]{1,0:T(8,128)(2,1)}, u32[]{:S(2)}) %copy-start) | copy-done | bytes 294936
  2.9 0.0 copy-start.1
  2.9 1.0 %copy-done.1 = bf16[128,1152]{1,0:T(8,128)(2,1)S(1)} copy-done((bf16[128,1152]{1,0:T(8,128)(2,1)S(1)}, bf16[128,1152]{1,0:T(8,128)(2,1)}, u32[]{:S(2)}) %copy-start.1) | copy-done | bytes 294936
  3.8 78.7 %shard_map.67 = (f32[1,128]{1,0:T(1,128)S(1)}, f32[128,1152]{1,0:T(8,128)S(1)}, f32[128,1152]{1,0:T(8,128)S(1)}) custom-call(f32[1]{0:T(128)S(6)} %copy.10.refs_0_, f32[1]{0:T(128)S(6)} %copy.11.refs_1_, bf16[128,1152]{1,0:T(8,128)(2,1)S(1)} %copy-done, bf16[128,1152]{1,0:T(8,128)(2,1)S(1)} %copy-done.1), custom_call_target="tpu_custom_call" | custom-call | tf_op jit(solution)/shard_map/pallas_call | solution.py:345
  82.6 0.5 copy.12
  83.1 0.8 copy.13
  83.9 0.8 copy.14
Async XLA Ops:
  1.9 1.0 %copy-start = (bf16[128,1152]{1,0:T(8,128)(2,1)S(1)}, bf16[128,1152]{1,0:T(8,128)(2,1)}, u32[]{:S(2)}) copy-start(bf16[128,1152]{1,0:T(8,128)(2,1)} %refs_2_.1) | copy-start | bytes 884740
  2.9 1.0 %copy-start.1 = (bf16[128,1152]{1,0:T(8,128)(2,1)S(1)}, bf16[128,1152]{1,0:T(8,128)(2,1)}, u32[]{:S(2)}) copy-start(bf16[128,1152]{1,0:T(8,128)(2,1)} %refs_3_.1) | copy-start | bytes 884740

commit v7 on v2

--- a/solution.py
+++ b/solution.py
@@ -7,6 +7,7 @@
 
 MESH = pl.DeviceIdType.MESH
 EPS = 1e-06
+LOG2_E = 1.4426950408889634
 
 X_N = 4
 Z_LO = 4
@@ -50,16 +51,15 @@
 
 
 def kernel(
-    groups, ls_ref, b_ref, img_ref, txt_ref, loss_ref, gi_ref, gt_ref,
-    texts, images, wt, tg, ig, loss_acc, relay, far_s, far_r, row_s, row_r, col_s, back, col_r,
-    sib_s, sib_r, sib_ls, sib_lr, ret_s, ret_r, ret_ls, ret_lr, ssem, rsem,
+    groups, ls_ref, b_ref, img_hbm, txt_hbm, loss_hbm, gi_hbm, gt_hbm,
+    img_ref, txt_ref, loss_ref, gi_ref, gt_ref, texts, images, wt, tg, ig, loss_acc, relay, far_s, far_r, row_s, row_r, col_s, back, col_r,
+    sib_s, sib_r, sib_ls, sib_lr, ret_s, ret_r, ret_ls, ret_lr, ssem, rsem, io_sem,
 ):
     rows, width = img_ref.shape
     sub = rows // CHUNKS
     half = sub // 2
     pair = 2 * rows
     unit = 4 * sub
-    tile = width // 3 if width % 384 == 0 else width
     peers = places(groups)
     messages = []
 
@@ -111,23 +111,27 @@
     ret = [message(ret_s.at[0], ret_r.at[1], "gp"), message(ret_s.at[1], ret_r.at[0], "gn")]
     ret_loss = [message(ret_ls.at[0], ret_lr.at[1], "gp"), message(ret_ls.at[1], ret_lr.at[0], "gn")]
 
-    barrier = pltpu.get_barrier_semaphore()
-    for peer in peers.values():
-        pl.semaphore_signal(barrier, inc=1, device_id=peer, device_id_type=MESH)
-
-    own = unit_of(txt_ref[...])[0].astype(jnp.bfloat16)
-    for c in range(CHUNKS):
-        texts[pl.ds(base(0, c), sub), :] = own[c * sub:(c + 1) * sub]
-    images[pl.ds(0, rows), :] = unit_of(img_ref[...])[0].astype(jnp.bfloat16)
-    loss_acc[...] = jnp.zeros_like(loss_acc)
-    scale = jnp.exp(jnp.full((1, pair), ls_ref[0], jnp.float32))
-    offset = b_ref[0]
-    pl.semaphore_wait(barrier, len(peers))
-
     def start(*pairs):
         for one in pairs:
             for copy in one:
                 copy.start()
+
+    fetch = [pltpu.make_async_copy(txt_hbm, txt_ref, io_sem.at[0]), pltpu.make_async_copy(img_hbm, img_ref, io_sem.at[1])]
+    start(fetch)
+    barrier = pltpu.get_barrier_semaphore()
+    for peer in peers.values():
+        pl.semaphore_signal(barrier, inc=1, device_id=peer, device_id_type=MESH)
+
+    fetch[0].wait()
+    own = unit_of(txt_ref[...])[0].astype(jnp.bfloat16)
+    for c in range(CHUNKS):
+        texts[pl.ds(base(0, c), sub), :] = own[c * sub:(c + 1) * sub]
+    fetch[1].wait()
+    images[pl.ds(0, rows), :] = unit_of(img_ref[...])[0].astype(jnp.bfloat16)
+    loss_acc[...] = jnp.zeros_like(loss_acc)
+    scale = jnp.exp(jnp.full((1, pair), ls_ref[0], jnp.float32)) * LOG2_E
+    offset = b_ref[0] * LOG2_E
+    pl.semaphore_wait(barrier, len(peers))
 
     def arrive(*pairs):
         for one in pairs:
@@ -140,16 +144,16 @@
             texts[pl.ds(start, unit), :], images[columns, :], (((1,), (1,)), ((), ())),
             preferred_element_type=jnp.float32,
         )
-        logits = scale * dots + offset
-        grown = jnp.exp(logits)
+        grown = jnp.exp2(scale * dots + offset)
         whole = 1.0 + grown
-        weights = grown / whole
+        inverse = pl.reciprocal(whole, approx=True)
+        weights = grown * (inverse * (2.0 - whole * inverse))
         if diagonal:
             row = lax.broadcasted_iota(jnp.int32, (unit, pair), 0)
             column = lax.broadcasted_iota(jnp.int32, (unit, pair), 1)
             positive = (row + c * sub == column) & (row < sub)
             weights = weights - positive.astype(jnp.float32)
-            whole = jnp.where(positive, 1.0 + jnp.exp(-logits), whole)
+            whole = jnp.where(positive, 1.0 + 1.0 / grown, whole)
         wt[pl.ds(start, unit), columns] = weights.astype(jnp.bfloat16)
         q = unit // 4
         product = (whole[:q] * whole[q:2 * q]) * (whole[2 * q:3 * q] * whole[3 * q:])
@@ -159,19 +163,14 @@
         begin = base(r, c)
         for j in range(3):
             weigh(c, begin, j, r == 0 and j == 0)
-        for n in range(width // tile):
-            columns = pl.ds(n * tile, tile)
-            tg[pl.ds(begin, unit), columns] = jnp.dot(
-                wt[pl.ds(begin, unit), :], images[:, columns], preferred_element_type=jnp.float32
-            )
+        tg[pl.ds(begin, unit), :] = jnp.dot(
+            wt[pl.ds(begin, unit), :], images[...], preferred_element_type=jnp.float32
+        )
 
     def image_partial(first):
-        for n in range(width // tile):
-            columns = pl.ds(n * tile, tile)
-            ig[pl.ds(first, 3 * rows), columns] = lax.dot_general(
-                wt[:, pl.ds(first, 3 * rows)], texts[:, columns], (((0,), (0,)), ((), ())),
-                preferred_element_type=jnp.float32,
-            )
+        ig[pl.ds(first, 3 * rows), :] = lax.dot_general(
+            wt[:, pl.ds(first, 3 * rows)], texts[...], (((0,), (0,)), ((), ())), preferred_element_type=jnp.float32
+        )
 
     def partial(r, c, k, h):
         return tg[pl.ds(base(r, c) + k * sub + h * half, half), :]
@@ -249,6 +248,7 @@
     for h in range(2):
         z_out[1][h].wait_recv()
         z_on[1][h].start()
+    reduce_begin(0, 0)
     far_forward(1, 0)
     all_here(0, 1)
     both(0, 1)
@@ -264,6 +264,7 @@
 
     reduce_begin(1, 1)
     column_home(0)
+    reduce_begin(0, 1)
     image_partial(3 * rows)
     for k in (1, 2, 0):
         sib_s[k] = ig[pl.ds((3 + k) * rows, rows), :].astype(jnp.bfloat16)
@@ -286,12 +287,10 @@
         ret_ls[s] = jnp.broadcast_to(loss_of(s + 1) + sib_lr[pl.ds(s + 1, 1), :], ret_ls.shape[1:])
         ret_loss[s].start()
     for c in range(CHUNKS):
-        reduce_begin(0, c)
+        reduce_middle(0, c)
     for h in range(2):
         z_back[1][h].wait_recv()
         z_home[1][h].start()
-    for c in range(CHUNKS):
-        reduce_middle(0, c)
 
     scale_row = jnp.exp(jnp.full((1, width), ls_ref[0], jnp.float32))
 
@@ -299,12 +298,19 @@
         unit, inverse = unit_of(raw)
         grads = scale_row * grads
         return (grads - unit * jnp.sum(unit * grads, axis=1, keepdims=True)) * inverse
+
+    put = [pltpu.make_async_copy(loss_ref, loss_hbm, io_sem.at[2])]
+    for c in range(CHUNKS):
+        here = pl.ds(c * sub, sub)
+        put.append(pltpu.make_async_copy(gi_ref.at[here, :], gi_hbm.at[here, :], io_sem.at[3 + 2 * c]))
+        put.append(pltpu.make_async_copy(gt_ref.at[here, :], gt_hbm.at[here, :], io_sem.at[4 + 2 * c]))
 
     def finish_text(c):
         for h in range(2):
             near = reduce_end(0, c, h)
             z_home[c][h].wait_recv()
             gt_ref[piece(c, h), :] = backprop(txt_ref[piece(c, h), :], near + col_r[piece(c, h), :].astype(jnp.float32))
+        put[2 + 2 * c].start()
 
     finish_text(0)
     sib_back[0].wait_recv()
@@ -312,6 +318,7 @@
         ret_loss[s].wait_recv()
         ret[s].wait_recv()
     loss_ref[...] = loss_of(0) + sib_lr[pl.ds(0, 1), :] + ret_lr[0, pl.ds(0, 1), :] + ret_lr[1, pl.ds(0, 1), :]
+    put[0].start()
     for c in range(CHUNKS):
         for h in range(2):
             here = piece(c, h)
@@ -320,9 +327,21 @@
                 + (ret_r[0, here, :].astype(jnp.float32) + ret_r[1, here, :].astype(jnp.float32))
             )
             gi_ref[here, :] = backprop(img_ref[here, :], grads)
+        put[1 + 2 * c].start()
     finish_text(1)
     for sent in messages:
         sent.wait_send()
+    for copy in put:
+        copy.wait()
+
+
+def write_out(*refs):
+    sources, results, sem = refs[:3], refs[3:6], refs[6]
+    copies = [pltpu.make_async_copy(src, dst, sem.at[n]) for n, (src, dst) in enumerate(zip(sources, results))]
+    for copy in copies:
+        copy.start()
+    for copy in copies:
+        copy.wait()
 
 
 N_MESSAGES = 77
@@ -331,18 +350,24 @@
 def per_device(groups, image_emb, text_emb, log_scale, bias):
     rows, width = image_emb.shape
     half_type, full = jnp.bfloat16, jnp.float32
-    vmem = pl.BlockSpec(memory_space=pltpu.VMEM)
     smem = pl.BlockSpec(memory_space=pltpu.SMEM)
-    loss, grad_image, grad_text = pl.pallas_call(
+    anywhere = pl.BlockSpec(memory_space=pl.ANY)
+    out_shape = (
+        jax.ShapeDtypeStruct((1, rows), full),
+        jax.ShapeDtypeStruct((rows, width), full),
+        jax.ShapeDtypeStruct((rows, width), full),
+    )
+    results = pl.pallas_call(
         lambda *refs: kernel(groups, *refs),
-        out_shape=(
-            jax.ShapeDtypeStruct((1, rows), full),
-            jax.ShapeDtypeStruct((rows, width), full),
-            jax.ShapeDtypeStruct((rows, width), full),
-        ),
-        in_specs=[smem, smem, vmem, vmem],
-        out_specs=(vmem, vmem, vmem),
+        out_shape=out_shape,
+        in_specs=[smem, smem, anywhere, anywhere],
+        out_specs=(anywhere,) * 3,
         scratch_shapes=[
+            pltpu.VMEM((rows, width), half_type),
+            pltpu.VMEM((rows, width), half_type),
+            pltpu.VMEM((1, rows), full),
+            pltpu.VMEM((rows, width), full),
+            pltpu.VMEM((rows, width), full),
             pltpu.VMEM((8 * rows, width), half_type),
             pltpu.VMEM((6 * rows, width), half_type),
             pltpu.VMEM((8 * rows, 6 * rows), half_type),
@@ -367,11 +392,20 @@
             pltpu.VMEM((2, 8, rows), full),
             pltpu.SemaphoreType.DMA((N_MESSAGES,)),
             pltpu.SemaphoreType.DMA((N_MESSAGES,)),
+            pltpu.SemaphoreType.DMA((3 + 2 * CHUNKS,)),
         ],
         compiler_params=pltpu.CompilerParams(
-            collective_id=0, has_side_effects=True, vmem_limit_bytes=48 * 1024 * 1024
+            collective_id=0, has_side_effects=True, vmem_limit_bytes=60 * 1024 * 1024
         ),
     )(log_scale, bias, image_emb, text_emb)
+    loss, grad_image, grad_text = pl.pallas_call(
+        write_out,
+        out_shape=out_shape,
+        in_specs=[anywhere] * 3,
+        out_specs=(anywhere,) * 3,
+        scratch_shapes=[pltpu.SemaphoreType.DMA((3,))],
+        compiler_params=pltpu.CompilerParams(vmem_limit_bytes=60 * 1024 * 1024),
+    )(*results)
     return (loss.reshape(rows), grad_image, grad_text)
 
 

time: 81.2 us -> 117 us (1.44)
  the two profiles are of different devices: /device:TPU:72 before, /device:TPU:104 now
where the time goes in v7:
time: 117 us; the launch traced here: 116 us
  Pallas kernels  115 us (98%)
  between operations  1.93 us (2%)
    pallas_call x1, Pallas kernels, per_device(): pl.pallas_call(lambda *refs: kernel(groups, *refs), out_shape=out_shape,...  77.7 us
    pallas_call x1, Pallas kernels, per_device(): pl.pallas_call(write_out, out_shape=out_shape, in_specs=[anywhere] * 3, o...  36.9 us

profile of v7, /device:TPU:104, one launch (start us, length us, event | category | flops | bytes accessed | tf_op | source)
XLA Modules:
  0.0 116.5 jit_solution(4953875211252591556)
XLA Ops:
  1.9 77.7 %shard_map.67 = (f32[1,128]{1,0:T(1,128)}, f32[128,1152]{1,0:T(8,128)}, f32[128,1152]{1,0:T(8,128)}) custom-call(f32[1]{0:T(128)S(6)} %copy.7.refs_0_, f32[1]{0:T(128)S(6)} %copy.8.refs_1_, bf16[128,1152]{1,0:T(8,128)(2,1)} %refs_2_.1, bf16[128,1152]{1,0:T(8,128)(2,1)} %refs_3_.1), custom_call_target="tpu_custom_call" | custom-call | tf_op jit(solution)/shard_map/pallas_call | solution.py:360
  79.6 36.9 %shard_map.68 = (f32[1,128]{1,0:T(1,128)}, f32[128,1152]{1,0:T(8,128)}, f32[128,1152]{1,0:T(8,128)}) custom-call(f32[1,128]{1,0:T(1,128)} %get-tuple-element.9.refs_0_, f32[128,1152]{1,0:T(8,128)} %get-tuple-element.10.refs_1_, f32[128,1152]{1,0:T(8,128)} %get-tuple-element.11.refs_2_), custom_call_target="tpu_custom_call" | custom-call | tf_op jit(solution)/shard_map/pallas_call | solution.py:401

commit v8 on v6

--- a/solution.py
+++ b/solution.py
@@ -18,6 +18,8 @@
 
 CHUNKS = 2
 PARTS = 1
+SPLIT = 4
+SMALLEST = 16
 
 
 def unit_of(raw):
@@ -49,6 +51,32 @@
         "tn": group_by(2),
         "tp": group_by(-2),
     }
+
+
+class Message:
+    def __init__(self, src, dst, peer, ssem, rsem, first):
+        n = src.shape[-2]
+        count = max(1, min(SPLIT, n // SMALLEST))
+        size = n // count
+        self.copies = [
+            pltpu.make_async_remote_copy(
+                src_ref=src.at[pl.ds(i * size, size), :], dst_ref=dst.at[pl.ds(i * size, size), :],
+                send_sem=ssem.at[first + i], recv_sem=rsem.at[first + i], device_id=peer, device_id_type=MESH,
+            )
+            for i in range(count)
+        ]
+
+    def start(self):
+        for copy in self.copies:
+            copy.start()
+
+    def wait_recv(self):
+        for copy in self.copies:
+            copy.wait_recv()
+
+    def wait_send(self):
+        for copy in self.copies:
+            copy.wait_send()
 
 
 def kernel(
@@ -67,13 +95,7 @@
     messages = []
 
     def message(src, dst, peer):
-        index = len(messages)
-        messages.append(
-            pltpu.make_async_remote_copy(
-                src_ref=src, dst_ref=dst, send_sem=ssem.at[index], recv_sem=rsem.at[index],
-                device_id=peers[peer], device_id_type=MESH,
-            )
-        )
+        messages.append(Message(src, dst, peers[peer], ssem, rsem, sum(len(one.copies) for one in messages)))
         return messages[-1]
 
     def at(c, k, h=0):
@@ -333,7 +355,7 @@
         sent.wait_send()
 
 
-N_MESSAGES = 46
+N_COPIES = 160
 
 
 def per_device(groups, image_emb, text_emb, log_scale, bias):
@@ -376,8 +398,8 @@
             pltpu.VMEM((2, 8, rows), full),
             pltpu.VMEM((2, 8, rows), full),
             pltpu.VMEM((2, 8, rows), full),
-            pltpu.SemaphoreType.DMA((N_MESSAGES,)),
-            pltpu.SemaphoreType.DMA((N_MESSAGES,)),
+            pltpu.SemaphoreType.DMA((N_COPIES,)),
+            pltpu.SemaphoreType.DMA((N_COPIES,)),
         ],
         compiler_params=pltpu.CompilerParams(
             collective_id=0, has_side_effects=True, vmem_limit_bytes=48 * 1024 * 1024

time: 84.9 us -> 87.2 us (1.027)
  Pallas kernels: 78.7 us -> 81 us
    pallas_call x1, Pallas kernels: 78.7 us -> 81 us  [per_device(): pl.pallas_call(lambda *refs: kernel(groups, *refs), out_shape=(jax.ShapeD...]
where the time goes in v8:
time: 87.2 us; the launch traced here: 87 us
  Pallas kernels  81 us (93%)
  local copies, waits for them, and re-layouts  4.06 us (5%)
  between operations  1.94 us (2%)
    pallas_call x1, Pallas kernels, per_device(): pl.pallas_call(lambda *refs: kernel(groups, *refs), out_shape=(jax.ShapeD...  81 us
    unnamed x7, local copies, waits for them, and re-layouts  4.06 us

profile of v8, /device:TPU:2, one launch (start us, length us, event | category | flops | bytes accessed | tf_op | source)
XLA Modules:
  0.0 87.0 jit_solution(9281928763377107450)
XLA Ops:
  1.9 0.0 copy-start
  1.9 1.0 %copy-done = bf16[128,1152]{1,0:T(8,128)(2,1)S(1)} copy-done((bf16[128,1152]{1,0:T(8,128)(2,1)S(1)}, bf16[128,1152]{1,0:T(8,128)(2,1)}, u32[]{:S(2)}) %copy-start) | copy-done | bytes 294936
  2.9 0.0 copy-start.1
  2.9 1.0 %copy-done.1 = bf16[128,1152]{1,0:T(8,128)(2,1)S(1)} copy-done((bf16[128,1152]{1,0:T(8,128)(2,1)S(1)}, bf16[128,1152]{1,0:T(8,128)(2,1)}, u32[]{:S(2)}) %copy-start.1) | copy-done | bytes 294936
  3.8 81.0 %shard_map.67 = (f32[1,128]{1,0:T(1,128)S(1)}, f32[128,1152]{1,0:T(8,128)S(1)}, f32[128,1152]{1,0:T(8,128)S(1)}) custom-call(f32[1]{0:T(128)S(6)} %copy.10.refs_0_, f32[1]{0:T(128)S(6)} %copy.11.refs_1_, bf16[128,1152]{1,0:T(8,128)(2,1)S(1)} %copy-done, bf16[128,1152]{1,0:T(8,128)(2,1)S(1)} %copy-done.1), custom_call_target="tpu_custom_call" | custom-call | tf_op jit(solution)/shard_map/pallas_call | solution.py:367
  84.8 0.5 copy.12
  85.3 0.8 copy.13
  86.1 0.8 copy.14
Async XLA Ops:
  1.9 1.0 %copy-start = (bf16[128,1152]{1,0:T(8,128)(2,1)S(1)}, bf16[128,1152]{1,0:T(8,128)(2,1)}, u32[]{:S(2)}) copy-start(bf16[128,1152]{1,0:T(8,128)(2,1)} %refs_2_.1) | copy-start | bytes 884740
  2.9 1.0 %copy-start.1 = (bf16[128,1152]{1,0:T(8,128)(2,1)S(1)}, bf16[128,1152]{1,0:T(8,128)(2,1)}, u32[]{:S(2)}) copy-start(bf16[128,1152]{1,0:T(8,128)(2,1)} %refs_3_.1) | copy-start | bytes 884740

commit v9 on v6

--- a/solution.py
+++ b/solution.py
@@ -53,8 +53,8 @@
 
 def kernel(
     groups, ls_ref, b_ref, img_ref, txt_ref, loss_ref, gi_ref, gt_ref,
-    texts, images, wt, tg, ig, loss_acc, over_s, over_r, three_s, three_r, one_s, one_r,
-    sib_s, sib_r, far_s, far_r, row_s, row_r, over_ls, over_lr, three_ls, three_lr, one_ls, one_lr, ssem, rsem,
+    texts, images, wt, tg, ig, loss_acc, five_s, five_r, over_s, over_r, three_s, three_r, one_s, one_r,
+    sib_s, sib_r, far_s, far_r, row_s, row_r, five_ls, five_lr, over_ls, over_lr, three_ls, three_lr, one_ls, one_lr, ssem, rsem,
 ):
     rows, width = img_ref.shape
     sub = rows // CHUNKS
@@ -103,10 +103,21 @@
     def edges(p, e):
         return pl.ds(p * part + e * edge, edge)
 
-    z1 = [[message(image(c, OWN), image(c, UP1), "gn"), message(image(c, OWN), image(c, DOWN1), "gp")] for c in range(CHUNKS)]
-    z3 = [[message(image(c, UP1), image(c, UP3), "tn"), message(image(c, DOWN1), image(c, DOWN3), "tp")] for c in range(CHUNKS)]
+    z1 = [[message(image_half(c, OWN, h), image_half(c, (UP1, DOWN1)[h], h), ("gn", "gp")[h]) for h in range(2)] for c in range(CHUNKS)]
+    z1_other = [
+        [message(image_half(c, OWN, 1 - h), image_half(c, (UP1, DOWN1)[h], 1 - h), ("gn", "gp")[h]) for h in range(2)]
+        for c in range(CHUNKS)
+    ]
+    z3 = [
+        [message(image_half(c, (UP1, DOWN1)[h], h), image_half(c, (UP3, DOWN3)[h], h), ("tn", "tp")[h]) for h in range(2)]
+        for c in range(CHUNKS)
+    ]
     z4 = [
-        [message(image_half(c, UP3, 0), image_half(c, OVER, 0), "gn"), message(image_half(c, DOWN3, 1), image_half(c, OVER, 1), "gp")]
+        [message(image_half(c, (UP3, DOWN3)[h], h), image_half(c, OVER, h), ("gn", "gp")[h]) for h in range(2)]
+        for c in range(CHUNKS)
+    ]
+    z5 = [
+        [message(image_half(c, OVER, h), image_half(c, (DOWN3, UP3)[h], h), ("gn", "gp")[h]) for h in range(2)]
         for c in range(CHUNKS)
     ]
     x1 = [[message(text_part(OWN, p), text_part((PREV, NEXT)[s], p), ("xn", "xp")[s]) for s in range(2)] for p in range(PARTS)]
@@ -115,12 +126,18 @@
         for p in range(PARTS)
     ]
     across = [message(text(0, j), text(1, j), "sib") for j in range(4)]
+    b5 = [[message(five_s.at[c, halves(h), :], five_r.at[c, halves(h), :], ("gp", "gn")[h]) for h in range(2)] for c in range(CHUNKS)]
     b4 = [[message(over_s.at[c, halves(h), :], over_r.at[c, halves(h), :], ("gp", "gn")[h]) for h in range(2)] for c in range(CHUNKS)]
-    b3 = [[message(three_s.at[c, h], three_r.at[c, h], ("tp", "tn")[h]) for h in range(2)] for c in range(CHUNKS)]
-    b1 = [[message(one_s.at[c, h], one_r.at[c, h], ("gp", "gn")[h]) for h in range(2)] for c in range(CHUNKS)]
+    b3 = [[message(three_s.at[c, halves(h), :], three_r.at[c, halves(h), :], ("tp", "tn")[h]) for h in range(2)] for c in range(CHUNKS)]
+    b1 = [[message(one_s.at[c, h, halves(h), :], one_r.at[c, h, halves(h), :], ("gp", "gn")[h]) for h in range(2)] for c in range(CHUNKS)]
+    b1_other = [
+        [message(one_s.at[c, h, halves(1 - h), :], one_r.at[c, h, halves(1 - h), :], ("gp", "gn")[h]) for h in range(2)]
+        for c in range(CHUNKS)
+    ]
     back = [[message(sib_s.at[j, parts(p), :], sib_r.at[j, parts(p), :], "sib") for j in range(4)] for p in range(PARTS)]
     t2 = [[message(far_s.at[edges(p, s), :], far_r.at[edges(p, s), :], ("xp", "xn")[s]) for s in range(2)] for p in range(PARTS)]
     t1 = [[message(row_s.at[s, parts(p), :], row_r.at[s, parts(p), :], ("xp", "xn")[s]) for s in range(2)] for p in range(PARTS)]
+    l5 = [message(five_ls.at[h], five_lr.at[h], ("gp", "gn")[h]) for h in range(2)]
     l4 = [message(over_ls, over_lr.at[h], ("gp", "gn")[h]) for h in range(2)]
     l3 = [message(three_ls.at[h], three_lr.at[h], ("tp", "tn")[h]) for h in range(2)]
     l1 = [message(one_ls.at[h], one_lr.at[h], ("gp", "gn")[h]) for h in range(2)]
@@ -199,25 +216,36 @@
     def gradient(c, k):
         return ig[pl.ds(at(c, k), sub), :]
 
-    def begin_back(c):
-        over_s[c] = gradient(c, OVER).astype(jnp.bfloat16)
-        start(b4[c])
-
-    def middle_back(c):
+    def send_back(sent, copies, c, h, k, came=None):
+        total = ig[pl.ds(at(c, k, h), half), :]
+        if came is not None:
+            total = total + came.astype(jnp.float32)
+        sent[halves(h), :] = total.astype(jnp.bfloat16)
+        copies[c][h].start()
+
+    def back_5(c):
+        for h in range(2):
+            send_back(five_s.at[c], b5, c, h, (DOWN3, UP3)[h])
+
+    def back_4(c):
+        for h in range(2):
+            b5[c][h].wait_recv()
+            send_back(over_s.at[c], b4, c, h, OVER, five_r[c, halves(h), :])
+
+    def back_3(c):
         for h in range(2):
             b4[c][h].wait_recv()
-            k = (UP3, DOWN3)[h]
-            came = pl.ds(at(c, k, h), half)
-            kept = pl.ds(at(c, k, 1 - h), half)
-            three_s[c, h, halves(h), :] = (ig[came, :] + over_r[c, halves(h), :].astype(jnp.float32)).astype(jnp.bfloat16)
-            three_s[c, h, halves(1 - h), :] = ig[kept, :].astype(jnp.bfloat16)
-            b3[c][h].start()
-
-    def end_back(c):
+            send_back(three_s.at[c], b3, c, h, (UP3, DOWN3)[h], over_r[c, halves(h), :])
+
+    def back_1(c):
         for h in range(2):
             b3[c][h].wait_recv()
-            one_s[c, h] = (gradient(c, (UP1, DOWN1)[h]) + three_r[c, h].astype(jnp.float32)).astype(jnp.bfloat16)
-            b1[c][h].start()
+            send_back(one_s.at[c, h], b1, c, h, (UP1, DOWN1)[h], three_r[c, halves(h), :])
+
+    def back_1_other(c):
+        for h in range(2):
+            one_s[c, h, halves(1 - h), :] = ig[pl.ds(at(c, (UP1, DOWN1)[h], 1 - h), half), :].astype(jnp.bfloat16)
+            b1_other[c][h].start()
 
     def loss_of(k):
         block = jnp.concatenate([loss_acc[pl.ds(at(c, k), sub), :] for c in range(CHUNKS)], axis=0)
@@ -247,61 +275,72 @@
 
     for c in range(CHUNKS):
         start(z1[c])
-    for p in range(PARTS):
-        start(x1[p])
+    start(x1[0])
     across[OWN].start()
+    for c in range(CHUNKS):
+        start(z1_other[c])
     pass_on(z1[0], z3[0])
-    for p in range(PARTS):
-        pass_on(x1[p], x2[p])
+    pass_on(z1[1], z3[1])
+    pass_on(x1[0], x2[0])
     across[PREV].start()
     across[NEXT].start()
-    pass_on(z1[1], z3[1])
+    for c in range(CHUNKS):
+        arrive(z1_other[c])
     wholes = [weigh(0, 3 * rows, 1, False)]
     arrive([across[PREV], across[NEXT]])
     wholes.append(weigh(0, 3 * rows, 3, False))
-    for p in range(PARTS):
-        arrive(x2[p])
+    arrive(x2[0])
     across[FAR].start()
     wholes.append(weigh(0, 3 * rows, 0, True))
     arrive([across[OWN], across[FAR]])
+    pass_on(z3[0], z4[0])
     wholes.append(weigh(0, 3 * rows, 2, False))
     loss_part(0, 3 * rows, wholes)
-    pass_on(z3[0], z4[0])
+    pass_on(z3[1], z4[1])
     image_partial(0, 3 * rows)
-    pass_on(z3[1], z4[1])
-    for q in (1, 0):
-        text_partial(0, q)
-    for c in range(CHUNKS):
-        arrive(z4[c])
+    pass_on(z4[0], z5[0])
+    text_partial(0, 1)
+    pass_on(z4[1], z5[1])
+    text_partial(0, 0)
+    for c in range(CHUNKS):
+        arrive(z5[c])
         far(c)
-        begin_back(c)
-
-    middle_back(0)
+        back_5(c)
+
+    back_4(0)
+    for c in range(CHUNKS):
+        back_1_other(c)
     text_partial(1, 1)
-    for p in range(PARTS):
-        for j in (FAR, PREV, NEXT, OWN):
-            sib_s[j, parts(p), :] = tg[pl.ds(row_texts + j * rows + p * part, part), :].astype(jnp.bfloat16)
-            back[p][j].start()
-    middle_back(1)
-    give_loss(over_ls, loss_of(OVER))
+    for j in (FAR, PREV, NEXT, OWN):
+        sib_s[j] = tg[pl.ds(row_texts + j * rows, rows), :].astype(jnp.bfloat16)
+        back[0][j].start()
+    back_4(1)
+    for h in range(2):
+        give_loss(five_ls.at[h], loss_of((DOWN3, UP3)[h]))
+        l5[h].start()
+    text_partial(1, 0)
+    back_3(0)
+    text_begin(0)
+    lane = lax.broadcasted_iota(jnp.int32, (1, rows), 1)
+
+    def of_half(h, came):
+        return jnp.where((lane // half) % 2 == h, came[h, pl.ds(0, 1), :], 0.0)
+
+    arrive(l5)
+    give_loss(over_ls, loss_of(OVER) + of_half(0, five_lr) + of_half(1, five_lr))
     start(l4)
-    text_partial(1, 0)
-    for p in range(PARTS):
-        text_begin(p)
-    end_back(0)
-    lane = lax.broadcasted_iota(jnp.int32, (1, rows), 1)
+    back_3(1)
+    text_middle(0)
     for h in range(2):
         l4[h].wait_recv()
-        mine = (lane // half) % 2 == h
-        give_loss(three_ls.at[h], loss_of((UP3, DOWN3)[h]) + jnp.where(mine, over_lr[h, pl.ds(0, 1), :], 0.0))
+        give_loss(three_ls.at[h], loss_of((UP3, DOWN3)[h]) + of_half(h, over_lr))
         l3[h].start()
-    for p in range(PARTS):
-        text_middle(p)
-    end_back(1)
+    back_1(0)
     for h in range(2):
         l3[h].wait_recv()
-        give_loss(one_ls.at[h], loss_of((UP1, DOWN1)[h]) + three_lr[h, pl.ds(0, 1), :])
+        give_loss(one_ls.at[h], loss_of((UP1, DOWN1)[h]) + of_half(h, three_lr))
         l1[h].start()
+    back_1(1)
 
     scale_row = jnp.exp(jnp.full((1, width), ls_ref[0], jnp.float32))
 
@@ -313,6 +352,7 @@
     def finish_image(c):
         here = pl.ds(c * sub, sub)
         arrive(b1[c])
+        arrive(b1_other[c])
         grads = gradient(c, OWN) + (one_r[c, 0].astype(jnp.float32) + one_r[c, 1].astype(jnp.float32))
         gi_ref[here, :] = backprop(img_ref[here, :], grads)
 
@@ -333,7 +373,7 @@
         sent.wait_send()
 
 
-N_MESSAGES = 46
+N_MESSAGES = 64
 
 
 def per_device(groups, image_emb, text_emb, log_scale, bias):
@@ -360,8 +400,10 @@
             pltpu.VMEM((6 * rows, rows), full),
             pltpu.VMEM((CHUNKS, sub, width), half_type),
             pltpu.VMEM((CHUNKS, sub, width), half_type),
-            pltpu.VMEM((CHUNKS, 2, sub, width), half_type),
-            pltpu.VMEM((CHUNKS, 2, sub, width), half_type),
+            pltpu.VMEM((CHUNKS, sub, width), half_type),
+            pltpu.VMEM((CHUNKS, sub, width), half_type),
+            pltpu.VMEM((CHUNKS, sub, width), half_type),
+            pltpu.VMEM((CHUNKS, sub, width), half_type),
             pltpu.VMEM((CHUNKS, 2, sub, width), half_type),
             pltpu.VMEM((CHUNKS, 2, sub, width), half_type),
             pltpu.VMEM((4, rows, width), half_type),
@@ -370,6 +412,8 @@
             pltpu.VMEM((rows, width), half_type),
             pltpu.VMEM((2, rows, width), half_type),
             pltpu.VMEM((2, rows, width), half_type),
+            pltpu.VMEM((2, 8, rows), full),
+            pltpu.VMEM((2, 8, rows), full),
             pltpu.VMEM((8, rows), full),
             pltpu.VMEM((2, 8, rows), full),
             pltpu.VMEM((2, 8, rows), full),

time: 84.9 us -> 76.5 us (0.901)
  the two profiles are of different devices: /device:TPU:2 before, /device:TPU:24 now
where the time goes in v9:
time: 76.5 us; the launch traced here: 76.3 us
  Pallas kernels  70.3 us (92%)
  local copies, waits for them, and re-layouts  4.06 us (5%)
  between operations  1.94 us (3%)
    pallas_call x1, Pallas kernels, per_device(): pl.pallas_call(lambda *refs: kernel(groups, *refs), out_shape=(jax.ShapeD...  70.3 us
    unnamed x7, local copies, waits for them, and re-layouts  4.06 us

profile of v9, /device:TPU:24, one launch (start us, length us, event | category | flops | bytes accessed | tf_op | source)
XLA Modules:
  0.0 76.3 jit_solution(352095074701192527)
XLA Ops:
  1.9 0.0 copy-start
  1.9 1.0 %copy-done = bf16[128,1152]{1,0:T(8,128)(2,1)S(1)} copy-done((bf16[128,1152]{1,0:T(8,128)(2,1)S(1)}, bf16[128,1152]{1,0:T(8,128)(2,1)}, u32[]{:S(2)}) %copy-start) | copy-done | bytes 294936
  2.9 0.0 copy-start.1
  2.9 1.0 %copy-done.1 = bf16[128,1152]{1,0:T(8,128)(2,1)S(1)} copy-done((bf16[128,1152]{1,0:T(8,128)(2,1)S(1)}, bf16[128,1152]{1,0:T(8,128)(2,1)}, u32[]{:S(2)}) %copy-start.1) | copy-done | bytes 294936
  3.8 70.3 %shard_map.67 = (f32[1,128]{1,0:T(1,128)S(1)}, f32[128,1152]{1,0:T(8,128)S(1)}, f32[128,1152]{1,0:T(8,128)S(1)}) custom-call(f32[1]{0:T(128)S(6)} %copy.10.refs_0_, f32[1]{0:T(128)S(6)} %copy.11.refs_1_, bf16[128,1152]{1,0:T(8,128)(2,1)S(1)} %copy-done, bf16[128,1152]{1,0:T(8,128)(2,1)S(1)} %copy-done.1), custom_call_target="tpu_custom_call" | custom-call | tf_op jit(solution)/shard_map/pallas_call | solution.py:385
  74.1 0.5 copy.12
  74.6 0.8 %copy.13 = f32[128,1152]{1,0:T(8,128)} copy(f32[128,1152]{1,0:T(8,128)S(1)} %get-tuple-element.13) | data formatting | bytes 1179648
  75.5 0.8 %copy.14 = f32[128,1152]{1,0:T(8,128)} copy(f32[128,1152]{1,0:T(8,128)S(1)} %get-tuple-element.14) | data formatting | bytes 1179648
Async XLA Ops:
  1.9 1.0 %copy-start = (bf16[128,1152]{1,0:T(8,128)(2,1)S(1)}, bf16[128,1152]{1,0:T(8,128)(2,1)}, u32[]{:S(2)}) copy-start(bf16[128,1152]{1,0:T(8,128)(2,1)} %refs_2_.1) | copy-start | bytes 884740
  2.9 1.0 %copy-start.1 = (bf16[128,1152]{1,0:T(8,128)(2,1)S(1)}, bf16[128,1152]{1,0:T(8,128)(2,1)}, u32[]{:S(2)}) copy-start(bf16[128,1152]{1,0:T(8,128)(2,1)} %refs_3_.1) | copy-start | bytes 884740

commit v10 on v9

--- a/solution.py
+++ b/solution.py
@@ -161,7 +161,6 @@
     own = unit_of(img_ref[...])[0].astype(jnp.bfloat16)
     for c in range(CHUNKS):
         images[pl.ds(at(c, OWN), sub), :] = own[c * sub:(c + 1) * sub]
-    texts[pl.ds(0, rows), :] = unit_of(txt_ref[...])[0].astype(jnp.bfloat16)
     scale = jnp.exp(jnp.full((1, tile), ls_ref[0], jnp.float32)) * LOG2_E
     offset = b_ref[0] * LOG2_E
     pl.semaphore_wait(barrier, len(peers))
@@ -275,6 +274,7 @@
 
     for c in range(CHUNKS):
         start(z1[c])
+    texts[pl.ds(0, rows), :] = unit_of(txt_ref[...])[0].astype(jnp.bfloat16)
     start(x1[0])
     across[OWN].start()
     for c in range(CHUNKS):
@@ -293,9 +293,9 @@
     across[FAR].start()
     wholes.append(weigh(0, 3 * rows, 0, True))
     arrive([across[OWN], across[FAR]])
-    pass_on(z3[0], z4[0])
     wholes.append(weigh(0, 3 * rows, 2, False))
     loss_part(0, 3 * rows, wholes)
+    pass_on(z3[0], z4[0])
     pass_on(z3[1], z4[1])
     image_partial(0, 3 * rows)
     pass_on(z4[0], z5[0])
@@ -304,12 +304,13 @@
     text_partial(0, 0)
     for c in range(CHUNKS):
         arrive(z5[c])
+        if c == 0:
+            for early in range(CHUNKS):
+                back_1_other(early)
         far(c)
         back_5(c)
 
     back_4(0)
-    for c in range(CHUNKS):
-        back_1_other(c)
     text_partial(1, 1)
     for j in (FAR, PREV, NEXT, OWN):
         sib_s[j] = tg[pl.ds(row_texts + j * rows, rows), :].astype(jnp.bfloat16)
@@ -376,19 +377,29 @@
 N_MESSAGES = 64
 
 
+def write_out(*refs):
+    sources, results, sem = refs[:3], refs[3:6], refs[6]
+    copies = [pltpu.make_async_copy(src, dst, sem.at[n]) for n, (src, dst) in enumerate(zip(sources, results))]
+    for copy in copies:
+        copy.start()
+    for copy in copies:
+        copy.wait()
+
+
 def per_device(groups, image_emb, text_emb, log_scale, bias):
     rows, width = image_emb.shape
     sub = rows // CHUNKS
     half_type, full = jnp.bfloat16, jnp.float32
     vmem = pl.BlockSpec(memory_space=pltpu.VMEM)
     smem = pl.BlockSpec(memory_space=pltpu.SMEM)
-    loss, grad_image, grad_text = pl.pallas_call(
+    out_shape = (
+        jax.ShapeDtypeStruct((1, rows), full),
+        jax.ShapeDtypeStruct((rows, width), full),
+        jax.ShapeDtypeStruct((rows, width), full),
+    )
+    results = pl.pallas_call(
         lambda *refs: kernel(groups, *refs),
-        out_shape=(
-            jax.ShapeDtypeStruct((1, rows), full),
-            jax.ShapeDtypeStruct((rows, width), full),
-            jax.ShapeDtypeStruct((rows, width), full),
-        ),
+        out_shape=out_shape,
         in_specs=[smem, smem, vmem, vmem],
         out_specs=(vmem, vmem, vmem),
         scratch_shapes=[
@@ -427,6 +438,14 @@
             collective_id=0, has_side_effects=True, vmem_limit_bytes=48 * 1024 * 1024
         ),
     )(log_scale, bias, image_emb, text_emb)
+    anywhere = pl.BlockSpec(memory_space=pl.ANY)
+    loss, grad_image, grad_text = pl.pallas_call(
+        write_out,
+        out_shape=out_shape,
+        in_specs=[vmem] * 3,
+        out_specs=(anywhere,) * 3,
+        scratch_shapes=[pltpu.SemaphoreType.DMA((3,))],
+    )(*results)
     return (loss.reshape(rows), grad_image, grad_text)
 
 

time: 76.5 us -> 78.8 us (1.030)
  the two profiles are of different devices: /device:TPU:24 before, /device:TPU:6 now
where the time goes in v10:
time: 78.8 us; the launch traced here: 78.4 us
  Pallas kernels  72.3 us (92%)
  local copies, waits for them, and re-layouts  4.15 us (5%)
  between operations  1.95 us (2%)
    pallas_call x1, Pallas kernels, per_device(): pl.pallas_call(lambda *refs: kernel(groups, *refs), out_shape=out_shape,...  70 us
    unnamed x10, local copies, waits for them, and re-layouts  4.15 us
    pallas_call x1, Pallas kernels, per_device(): pl.pallas_call(write_out, out_shape=out_shape, in_specs=[vmem] * 3, out_s...  2.28 us

profile of v10, /device:TPU:6, one launch (start us, length us, event | category | flops | bytes accessed | tf_op | source)
XLA Modules:
  0.0 78.4 jit_solution(11649343417646201520)
XLA Ops:
  1.9 0.0 copy-start.2
  1.9 1.0 %copy-done.2 = bf16[128,1152]{1,0:T(8,128)(2,1)S(1)} copy-done((bf16[128,1152]{1,0:T(8,128)(2,1)S(1)}, bf16[128,1152]{1,0:T(8,128)(2,1)}, u32[]{:S(2)}) %copy-start.2) | copy-done | bytes 294936
  2.9 0.0 copy-start.3
  2.9 1.0 %copy-done.3 = bf16[128,1152]{1,0:T(8,128)(2,1)S(1)} copy-done((bf16[128,1152]{1,0:T(8,128)(2,1)S(1)}, bf16[128,1152]{1,0:T(8,128)(2,1)}, u32[]{:S(2)}) %copy-start.3) | copy-done | bytes 294936
  3.8 70.0 %shard_map.67 = (f32[1,128]{1,0:T(1,128)S(1)}, f32[128,1152]{1,0:T(8,128)S(1)}, f32[128,1152]{1,0:T(8,128)S(1)}) custom-call(f32[1]{0:T(128)S(6)} %copy.7.refs_0_, f32[1]{0:T(128)S(6)} %copy.8.refs_1_, bf16[128,1152]{1,0:T(8,128)(2,1)S(1)} %copy-done.2, bf16[128,1152]{1,0:T(8,128)(2,1)S(1)} %copy-done.3), custom_call_target="tpu_custom_call" | custom-call | tf_op jit(solution)/shard_map/pallas_call | solution.py:400
  73.8 0.0 copy-start
  73.8 0.8 %copy-done = f32[128,1152]{1,0:T(8,128)} copy-done((f32[128,1152]{1,0:T(8,128)}, f32[128,1152]{1,0:T(8,128)S(1)}, u32[]{:S(2)}) %copy-start) | copy-done | bytes 589848
  74.7 0.0 copy-start.1
  74.7 0.8 %copy-done.1 = f32[128,1152]{1,0:T(8,128)} copy-done((f32[128,1152]{1,0:T(8,128)}, f32[128,1152]{1,0:T(8,128)S(1)}, u32[]{:S(2)}) %copy-start.1) | copy-done | bytes 589848
  75.5 0.0 copy-start.4
  75.5 0.6 copy-done.4
  76.1 2.3 %shard_map.68 = (f32[1,128]{1,0:T(1,128)}, f32[128,1152]{1,0:T(8,128)}, f32[128,1152]{1,0:T(8,128)}) custom-call(f32[1,128]{1,0:T(1,128)} %copy-done.4, f32[128,1152]{1,0:T(8,128)} %copy-done, f32[128,1152]{1,0:T(8,128)} %copy-done.1), custom_call_target="tpu_custom_call" | custom-call | tf_op jit(solution)/shard_map/pallas_call | solution.py:442
Async XLA Ops:
  1.9 1.0 %copy-start.2 = (bf16[128,1152]{1,0:T(8,128)(2,1)S(1)}, bf16[128,1152]{1,0:T(8,128)(2,1)}, u32[]{:S(2)}) copy-start(bf16[128,1152]{1,0:T(8,128)(2,1)} %refs_2_.1) | copy-start | bytes 884740
  2.9 1.0 %copy-start.3 = (bf16[128,1152]{1,0:T(8,128)(2,1)S(1)}, bf16[128,1152]{1,0:T(8,128)(2,1)}, u32[]{:S(2)}) copy-start(bf16[128,1152]{1,0:T(8,128)(2,1)} %refs_3_.1) | copy-start | bytes 884740
  73.8 0.8 %copy-start = (f32[128,1152]{1,0:T(8,128)}, f32[128,1152]{1,0:T(8,128)S(1)}, u32[]{:S(2)}) copy-start(f32[128,1152]{1,0:T(8,128)S(1)} %get-tuple-element.10.refs_1_) | copy-start | bytes 1769476
  74.7 0.8 %copy-start.1 = (f32[128,1152]{1,0:T(8,128)}, f32[128,1152]{1,0:T(8,128)S(1)}, u32[]{:S(2)}) copy-start(f32[128,1152]{1,0:T(8,128)S(1)} %get-tuple-element.11.refs_2_) | copy-start | bytes 1769476
  75.5 0.6 copy-start.4

commit v11 on v9

--- a/solution.py
+++ b/solution.py
@@ -77,10 +77,12 @@
         return messages[-1]
 
     def at(c, k, h=0):
-        return (c * 3 + k % 3) * sub + (k // 3) * 3 * rows + h * half
-
-    def image(c, k):
-        return images.at[pl.ds(at(c, k), sub), :]
+        if k < UP3:
+            return (c * 3 + k) * sub + h * half
+        if k == OVER:
+            return 4 * rows + (c * 2 + h) * half
+        first = 3 * rows if (k == UP3) == (h == 0) else 5 * rows
+        return first + (c * 2 + (k == DOWN3)) * half
 
     def image_half(c, k, h):
         return images.at[pl.ds(at(c, k, h), half), :]
@@ -161,7 +163,6 @@
     own = unit_of(img_ref[...])[0].astype(jnp.bfloat16)
     for c in range(CHUNKS):
         images[pl.ds(at(c, OWN), sub), :] = own[c * sub:(c + 1) * sub]
-    texts[pl.ds(0, rows), :] = unit_of(txt_ref[...])[0].astype(jnp.bfloat16)
     scale = jnp.exp(jnp.full((1, tile), ls_ref[0], jnp.float32)) * LOG2_E
     offset = b_ref[0] * LOG2_E
     pl.semaphore_wait(barrier, len(peers))
@@ -197,8 +198,7 @@
         here = pl.ds(begin, size)
         ig[here, :] = jnp.dot(wt[here, :], texts[...], preferred_element_type=jnp.float32)
 
-    def far(c):
-        begin, size = at(c, UP3), 3 * sub
+    def far(begin, size):
         loss_part(begin, size, [weigh(begin, size, n, False) for n in range(4)])
         image_partial(begin, size)
 
@@ -248,7 +248,9 @@
             b1_other[c][h].start()
 
     def loss_of(k):
-        block = jnp.concatenate([loss_acc[pl.ds(at(c, k), sub), :] for c in range(CHUNKS)], axis=0)
+        block = jnp.concatenate(
+            [loss_acc[pl.ds(at(c, k, h), half), :] for c in range(CHUNKS) for h in range(2)], axis=0
+        )
         return jnp.sum(block.T, axis=0, keepdims=True)
 
     def give_loss(dst, row):
@@ -275,6 +277,7 @@
 
     for c in range(CHUNKS):
         start(z1[c])
+    texts[pl.ds(0, rows), :] = unit_of(txt_ref[...])[0].astype(jnp.bfloat16)
     start(x1[0])
     across[OWN].start()
     for c in range(CHUNKS):
@@ -293,23 +296,25 @@
     across[FAR].start()
     wholes.append(weigh(0, 3 * rows, 0, True))
     arrive([across[OWN], across[FAR]])
-    pass_on(z3[0], z4[0])
     wholes.append(weigh(0, 3 * rows, 2, False))
     loss_part(0, 3 * rows, wholes)
+    pass_on(z3[0], z4[0])
     pass_on(z3[1], z4[1])
     image_partial(0, 3 * rows)
     pass_on(z4[0], z5[0])
     text_partial(0, 1)
     pass_on(z4[1], z5[1])
+    far(3 * rows, 2 * rows)
+    arrive(z5[0])
+    for c in range(CHUNKS):
+        back_1_other(c)
+    arrive(z5[1])
+    far(5 * rows, rows)
+    for c in range(CHUNKS):
+        back_5(c)
+
     text_partial(0, 0)
-    for c in range(CHUNKS):
-        arrive(z5[c])
-        far(c)
-        back_5(c)
-
     back_4(0)
-    for c in range(CHUNKS):
-        back_1_other(c)
     text_partial(1, 1)
     for j in (FAR, PREV, NEXT, OWN):
         sib_s[j] = tg[pl.ds(row_texts + j * rows, rows), :].astype(jnp.bfloat16)
@@ -382,13 +387,14 @@
     half_type, full = jnp.bfloat16, jnp.float32
     vmem = pl.BlockSpec(memory_space=pltpu.VMEM)
     smem = pl.BlockSpec(memory_space=pltpu.SMEM)
+    out_shape = (
+        jax.ShapeDtypeStruct((1, rows), full),
+        jax.ShapeDtypeStruct((rows, width), full),
+        jax.ShapeDtypeStruct((rows, width), full),
+    )
     loss, grad_image, grad_text = pl.pallas_call(
         lambda *refs: kernel(groups, *refs),
-        out_shape=(
-            jax.ShapeDtypeStruct((1, rows), full),
-            jax.ShapeDtypeStruct((rows, width), full),
-            jax.ShapeDtypeStruct((rows, width), full),
-        ),
+        out_shape=out_shape,
         in_specs=[smem, smem, vmem, vmem],
         out_specs=(vmem, vmem, vmem),
         scratch_shapes=[

time: 76.5 us -> 76.5 us (level)
  the two profiles are of different devices: /device:TPU:24 before, /device:TPU:6 now
where the time goes in v11:
time: 76.5 us; the launch traced here: 76.3 us
  Pallas kernels  70.3 us (92%)
  local copies, waits for them, and re-layouts  4.06 us (5%)
  between operations  1.94 us (3%)
    pallas_call x1, Pallas kernels, per_device(): pl.pallas_call(lambda *refs: kernel(groups, *refs), out_shape=out_shape,...  70.3 us
    unnamed x7, local copies, waits for them, and re-layouts  4.06 us

profile of v11, /device:TPU:6, one launch (start us, length us, event | category | flops | bytes accessed | tf_op | source)
XLA Modules:
  0.0 76.3 jit_solution(14372076931288223165)
XLA Ops:
  1.9 0.0 copy-start
  1.9 1.0 %copy-done = bf16[128,1152]{1,0:T(8,128)(2,1)S(1)} copy-done((bf16[128,1152]{1,0:T(8,128)(2,1)S(1)}, bf16[128,1152]{1,0:T(8,128)(2,1)}, u32[]{:S(2)}) %copy-start) | copy-done | bytes 294936
  2.9 0.0 copy-start.1
  2.9 1.0 %copy-done.1 = bf16[128,1152]{1,0:T(8,128)(2,1)S(1)} copy-done((bf16[128,1152]{1,0:T(8,128)(2,1)S(1)}, bf16[128,1152]{1,0:T(8,128)(2,1)}, u32[]{:S(2)}) %copy-start.1) | copy-done | bytes 294936
  3.8 70.3 %shard_map.67 = (f32[1,128]{1,0:T(1,128)S(1)}, f32[128,1152]{1,0:T(8,128)S(1)}, f32[128,1152]{1,0:T(8,128)S(1)}) custom-call(f32[1]{0:T(128)S(6)} %copy.10.refs_0_, f32[1]{0:T(128)S(6)} %copy.11.refs_1_, bf16[128,1152]{1,0:T(8,128)(2,1)S(1)} %copy-done, bf16[128,1152]{1,0:T(8,128)(2,1)S(1)} %copy-done.1), custom_call_target="tpu_custom_call" | custom-call | tf_op jit(solution)/shard_map/pallas_call | solution.py:395
  74.2 0.5 copy.12
  74.7 0.8 %copy.13 = f32[128,1152]{1,0:T(8,128)} copy(f32[128,1152]{1,0:T(8,128)S(1)} %get-tuple-element.13) | data formatting | bytes 1179648
  75.5 0.8 %copy.14 = f32[128,1152]{1,0:T(8,128)} copy(f32[128,1152]{1,0:T(8,128)S(1)} %get-tuple-element.14) | data formatting | bytes 1179648
Async XLA Ops:
  1.9 1.0 %copy-start = (bf16[128,1152]{1,0:T(8,128)(2,1)S(1)}, bf16[128,1152]{1,0:T(8,128)(2,1)}, u32[]{:S(2)}) copy-start(bf16[128,1152]{1,0:T(8,128)(2,1)} %refs_2_.1) | copy-start | bytes 884740
  2.9 1.0 %copy-start.1 = (bf16[128,1152]{1,0:T(8,128)(2,1)S(1)}, bf16[128,1152]{1,0:T(8,128)(2,1)}, u32[]{:S(2)}) copy-start(bf16[128,1152]{1,0:T(8,128)(2,1)} %refs_3_.1) | copy-start | bytes 884740

commit v12 on v11

--- a/solution.py
+++ b/solution.py
@@ -275,9 +275,9 @@
             row_s[s, edges(p, s), :] = total.astype(jnp.bfloat16)
             t1[p][s].start()
 
-    for c in range(CHUNKS):
-        start(z1[c])
+    start(z1[0])
     texts[pl.ds(0, rows), :] = unit_of(txt_ref[...])[0].astype(jnp.bfloat16)
+    start(z1[1])
     start(x1[0])
     across[OWN].start()
     for c in range(CHUNKS):
@@ -308,10 +308,11 @@
     arrive(z5[0])
     for c in range(CHUNKS):
         back_1_other(c)
+    far(5 * rows, sub)
+    back_5(0)
     arrive(z5[1])
-    far(5 * rows, rows)
-    for c in range(CHUNKS):
-        back_5(c)
+    far(5 * rows + sub, sub)
+    back_5(1)
 
     text_partial(0, 0)
     back_4(0)

time: 76.5 us -> 76.7 us (level); the launches traced: 76.3 us -> 75.6 us
  no operation moved by 1% of the time
where the time goes in v12:
time: 76.7 us; the launch traced here: 75.6 us
  Pallas kernels  69.6 us (91%)
  local copies, waits for them, and re-layouts  4.06 us (5%)
  between operations  1.94 us (3%)
    pallas_call x1, Pallas kernels, per_device(): pl.pallas_call(lambda *refs: kernel(groups, *refs), out_shape=out_shape,...  69.6 us
    unnamed x7, local copies, waits for them, and re-layouts  4.06 us

profile of v12, /device:TPU:6, one launch (start us, length us, event | category | flops | bytes accessed | tf_op | source)
XLA Modules:
  0.0 75.6 jit_solution(13365100168528672679)
XLA Ops:
  1.9 0.0 copy-start
  1.9 1.0 %copy-done = bf16[128,1152]{1,0:T(8,128)(2,1)S(1)} copy-done((bf16[128,1152]{1,0:T(8,128)(2,1)S(1)}, bf16[128,1152]{1,0:T(8,128)(2,1)}, u32[]{:S(2)}) %copy-start) | copy-done | bytes 294936
  2.9 0.0 copy-start.1
  2.9 1.0 %copy-done.1 = bf16[128,1152]{1,0:T(8,128)(2,1)S(1)} copy-done((bf16[128,1152]{1,0:T(8,128)(2,1)S(1)}, bf16[128,1152]{1,0:T(8,128)(2,1)}, u32[]{:S(2)}) %copy-start.1) | copy-done | bytes 294936
  3.8 69.6 %shard_map.67 = (f32[1,128]{1,0:T(1,128)S(1)}, f32[128,1152]{1,0:T(8,128)S(1)}, f32[128,1152]{1,0:T(8,128)S(1)}) custom-call(f32[1]{0:T(128)S(6)} %copy.10.refs_0_, f32[1]{0:T(128)S(6)} %copy.11.refs_1_, bf16[128,1152]{1,0:T(8,128)(2,1)S(1)} %copy-done, bf16[128,1152]{1,0:T(8,128)(2,1)S(1)} %copy-done.1), custom_call_target="tpu_custom_call" | custom-call | tf_op jit(solution)/shard_map/pallas_call | solution.py:396
  73.4 0.5 copy.12
  74.0 0.8 %copy.13 = f32[128,1152]{1,0:T(8,128)} copy(f32[128,1152]{1,0:T(8,128)S(1)} %get-tuple-element.13) | data formatting | bytes 1179648
  74.8 0.8 %copy.14 = f32[128,1152]{1,0:T(8,128)} copy(f32[128,1152]{1,0:T(8,128)S(1)} %get-tuple-element.14) | data formatting | bytes 1179648
Async XLA Ops:
  1.9 1.0 %copy-start = (bf16[128,1152]{1,0:T(8,128)(2,1)S(1)}, bf16[128,1152]{1,0:T(8,128)(2,1)}, u32[]{:S(2)}) copy-start(bf16[128,1152]{1,0:T(8,128)(2,1)} %refs_2_.1) | copy-start | bytes 884740
  2.9 1.0 %copy-start.1 = (bf16[128,1152]{1,0:T(8,128)(2,1)S(1)}, bf16[128,1152]{1,0:T(8,128)(2,1)}, u32[]{:S(2)}) copy-start(bf16[128,1152]{1,0:T(8,128)(2,1)} %refs_3_.1) | copy-start | bytes 884740
